TPU v7x, 256 devices: a whole 4x4x8 slice. The times are simulated.
256 devices in a mesh: batch: 2 (over x_hi), rows: 128 (over z, y, x_lo, core).
Axes of the slice: x: 4 (x_hi: 2, x_lo: 2; x = x_hi * 2 + x_lo), y: 4, z: 8, core: 2. Of those that a mesh axis runs over, the one named last changes fastest.
Arguments:
- surface: bfloat16 [2, 64, 2048, 1024], P('batch', None, 'rows'), may hold values from -6 to 6
- cotangent: bfloat16 [2, 64, 2048, 1024], P('batch', None, 'rows'), may hold values from -6 to 6
- spectral_weight: bfloat16 [256, 2, 64, 64, 128], P('rows', None, None, None, 'batch'), may hold values from -3 to 3
- local_weight: bfloat16 [64, 64], replicated, may hold values from -0.75 to 0.75
- bias_vector: float32 [64], replicated, may hold values from -1 to 1
Outputs:
- surface_gradient: bfloat16 [2, 64, 2048, 1024], P('batch', None, 'rows')
- weight_gradient: float32 [256, 2, 64, 64, 128], P('rows', None, None, None, 'batch')
All inputs are finite; a program needn't handle non-finite values.
Results may differ from a plain program's by a relative error of at most 0.027.
Values may be sent and summed in bfloat16 or wider, within the bound.
A program may use at most 128 MiB of HBM per device.

v0:
```python
import math

import jax
import jax.numpy as jnp
import numpy as np
from jax import lax
from jax.experimental import pallas as pl
from jax.experimental.pallas import tpu as pltpu
from jax.sharding import PartitionSpec as P

MESH = pl.DeviceIdType.MESH
BF = jnp.bfloat16
F32 = jnp.float32

C = 64
R = 16
W = 1024
KW = 256
KH = 128
NZ = 8
NQ = 16
NI = 4
ROWS = C * R
CHUNK = NQ * R


def tables():
    w = np.arange(W)[:, None]
    k = np.arange(KW)[None, :]
    angle = 2 * np.pi * ((w * k) % W) / W
    columns = np.concatenate([np.cos(angle), -np.sin(angle)], axis=1)
    height = NZ * NQ * R
    jj = np.arange(KH // 2)
    rows = np.zeros((NZ, 2 * CHUNK, 2 * KH))
    for z in range(NZ):
        h = (z * CHUNK + np.arange(CHUNK))[:, None]
        for half in range(2):
            f = (jj - half * (KH // 2))[None, :]
            angle = 2 * np.pi * ((f * h) % height) / height
            cos, sin = np.cos(angle), np.sin(angle)
            at = half * KH
            rows[z, :CHUNK, at : at + 64] = cos
            rows[z, :CHUNK, at + 64 : at + 128] = -sin
            rows[z, CHUNK:, at : at + 64] = sin
            rows[z, CHUNK:, at + 64 : at + 128] = cos
    return columns, rows


def permutations():
    gather = np.zeros((128, NI, NZ, 32))
    spread = np.zeros((128, 2, C))
    modes = np.zeros((NI, 32, NQ, NI, 2))
    for q in range(NQ):
        for i in range(NI):
            for kk in range(2):
                row = q * 8 + i * 2 + kk
                gather[row, i, :, 2 * q + kk] = 1
                spread[row, kk, 16 * i + q] = 1
                modes[i, 2 * q + kk, q, i, kk] = 1
    gather = gather.reshape(128, 1024)
    spread = spread.reshape(128, 128)
    return gather, spread, modes.reshape(128, 128), spread.T.copy()


def dot(a, b, ca=1, cb=0):
    return lax.dot_general(a, b, (((ca,), (cb,)), ((), ())), preferred_element_type=F32)


def gelu_slope(v):
    cumulative = 0.5 * (1.0 + lax.erf(v * (1.0 / math.sqrt(2.0))))
    density = jnp.exp(-0.5 * v * v) * (1.0 / math.sqrt(2.0 * math.pi))
    return cumulative + v * density


def expand_matrix(start):
    row = lax.broadcasted_iota(jnp.int32, (CHUNK, C), 0) + start
    col = lax.broadcasted_iota(jnp.int32, (CHUNK, C), 1)
    return (row // R == col).astype(F32).astype(BF)


def same_row_mask():
    row = lax.broadcasted_iota(jnp.int32, (CHUNK, CHUNK), 0) % R
    col = lax.broadcasted_iota(jnp.int32, (CHUNK, CHUNK), 1) % R
    return row == col


def mix_rows(weight_rows):
    mask = same_row_mask()
    for i in range(NI):
        spread = dot(weight_rows, expand_matrix(i * CHUNK), 1, 1)
        yield i, jnp.where(mask, spread, 0.0).astype(BF)


def column_scale():
    lane = lax.broadcasted_iota(jnp.int32, (1, KW), 1)
    return jnp.where(lane == 0, 2.0**-21, 2.0**-20).astype(F32)


def half_sign():
    lane = lax.broadcasted_iota(jnp.int32, (1, 128), 1)
    return jnp.where(lane < 64, -1.0, 1.0).astype(F32)


def transfers(
    x_hbm, cot_hbm, w_hbm, t1_hbm, t1t_hbm, rows_hbm, lw_ref, bias_ref, gather_ref, spread_ref, modes_ref, natural_ref,
    slopes_hbm, back_hbm, xm_hbm, gm_hbm,
    x, cot, w, t1, t1t, rt, w2r, w2i, kron, pre, slopes,
    a_out, a_in, b_out, b_in, c_out, c_in, d_out, d_in, e_out, e_in, f_out, f_in, turned, mixed, nat,
    load, store, sa, ra, sb, rb, sc, rc, sd, rd, se, re, sf, rf,
):
    b = lax.axis_index("batch")
    d = lax.axis_index("rows")
    z = d // NQ
    q = d % NQ

    def in_plane(p):
        return lax.rem(q + p, NQ)

    def along(p):
        return lax.rem(z + p, NZ)

    def wait(ref, sem):
        pltpu.make_async_copy(ref, ref, sem).wait()

    def send(src, dst, s, r, batch, row):
        pltpu.make_async_remote_copy(
            src_ref=src, dst_ref=dst, send_sem=s, recv_sem=r, device_id=(batch, row), device_id_type=MESH
        ).start()

    def loop(lo, hi, body):
        def step(p, carry):
            body(p)
            return carry

        lax.fori_loop(lo, hi, step, 0)

    loads = []
    for i in range(NI):
        part = pl.ds(i * CHUNK, CHUNK)
        loads.append(pltpu.make_async_copy(x_hbm.at[part], x.at[part], load.at[i]))
    load_t1 = pltpu.make_async_copy(t1_hbm, t1, load.at[4])
    load_rows = pltpu.make_async_copy(rows_hbm.at[z], rt, load.at[5])
    load_w = pltpu.make_async_copy(w_hbm, w, load.at[6])
    load_t1t = pltpu.make_async_copy(t1t_hbm, t1t, load.at[7])
    load_cot = pltpu.make_async_copy(cot_hbm, cot, load.at[8])
    load_t1.start()
    for copy in loads:
        copy.start()
    for copy in (load_rows, load_w, load_t1t, load_cot):
        copy.start()

    barrier = pltpu.get_barrier_semaphore()

    def greet(batch, row):
        pl.semaphore_signal(barrier, inc=1, device_id=(batch, row), device_id_type=MESH)

    loop(1, NQ, lambda p: greet(b, z * NQ + in_plane(p)))
    loop(0, NQ, lambda p: greet(1 - b, z * NQ + p))
    loop(1, NZ, lambda p: greet(b, along(p) * NQ + q))
    pl.semaphore_wait(barrier, 2 * NQ - 1 + NZ - 1)

    def send_plane(out, into, s, r, rnd, i):
        def one(p):
            to = in_plane(p)
            send(out.at[rnd, i, to], into.at[rnd, i, q], s.at[rnd, i], r.at[rnd, i], b, z * NQ + to)

        loop(1, NQ, one)
        pltpu.make_async_copy(out.at[rnd, i, q], into.at[rnd, i, q], r.at[rnd, i]).start()

    def send_owners(out, into, s, r, rnd):
        def same(p):
            to = in_plane(p)
            send(out.at[rnd, b, to], into.at[rnd, b, q], s.at[rnd, 0], r.at[rnd], b, z * NQ + to)

        def other(p):
            to = in_plane(p)
            send(out.at[rnd, 1 - b, to], into.at[rnd, b, q], s.at[rnd, 1], r.at[rnd], 1 - b, z * NQ + to)

        loop(0, NQ, other)
        loop(1, NQ, same)
        pltpu.make_async_copy(out.at[rnd, b, q], into.at[rnd, b, q], r.at[rnd]).start()

    def to_modes(rnd, i):
        wait(a_in.at[rnd, i], ra.at[rnd, i])
        plane = a_in[rnd, i].reshape(CHUNK, 2 * KW)
        term = dot(plane[:, :KW], rt[:CHUNK], 0, 0) + dot(plane[:, KW:], rt[CHUNK:], 0, 0)
        b_out[rnd, i] = term.astype(BF).reshape(NZ, 32, 2 * KH)

        def one(p):
            to = along(p)
            send(b_out.at[rnd, i, to], b_in.at[rnd, i, z], sb.at[rnd, i], rb.at[rnd], b, to * NQ + q)

        loop(1, NZ, one)
        pltpu.make_async_copy(b_out.at[rnd, i, z], b_in.at[rnd, i, z], rb.at[rnd]).start()

    def to_owners(rnd):
        wait(b_in.at[rnd], rb.at[rnd])
        total = dot(gather_ref[...], b_in[rnd].reshape(1024, 2 * KH))
        for half in range(2):
            c_out[rnd, half] = total[:, half * KH : (half + 1) * KH].reshape(NQ, 8, KH)
        send_owners(c_out, c_in, sc, rc, rnd)

    def from_owners(rnd):
        for m in range(2):
            d_out[rnd, m] = dot(spread_ref[...], mixed[m].astype(BF)).reshape(NQ, 8, KH)
        send_owners(d_out, d_in, sd, rd, rnd)
        wait(d_in.at[rnd], rd.at[rnd])
        halves = [dot(modes_ref[...], d_in[rnd, half].reshape(128, KH).astype(BF)) for half in range(2)]
        e_out[rnd] = jnp.concatenate(halves, axis=1).astype(BF).reshape(NI, 32, 2 * KH)

        def spread_modes(i):
            def one(p):
                send(e_out.at[rnd, i], e_in.at[rnd, i, z], se.at[rnd, i], re.at[rnd, i], b, along(p) * NQ + q)

            loop(1, NZ, one)
            pltpu.make_async_copy(e_out.at[rnd, i], e_in.at[rnd, i, z], re.at[rnd, i]).start()

        loop(0, NI, spread_modes)

        def to_rows(i):
            wait(e_in.at[rnd, i], re.at[rnd, i])
            spectra = e_in[rnd, i].reshape(KW, 2 * KH)
            real = dot(rt[:CHUNK], spectra, 1, 1)
            imag = dot(rt[CHUNK:], spectra, 1, 1)
            if rnd == 0:
                real = real * column_scale()
                imag = imag * column_scale()
            f_out[rnd, i] = jnp.concatenate([real, imag], axis=1).astype(BF).reshape(NQ, R, 2 * KW)
            send_plane(f_out, f_in, sf, rf, rnd, i)

        loop(0, NI, to_rows)

    load_t1.wait()

    def first(i):
        part = pl.ds(pl.multiple_of(i * CHUNK, CHUNK), CHUNK)
        pltpu.make_async_copy(x_hbm.at[part], x.at[part], load.at[i]).wait()
        a_out[0, i] = dot(x[part], t1[...]).astype(BF).reshape(NQ, R, 2 * KW)
        send_plane(a_out, a_in, sa, ra, 0, i)

    loop(0, NI, first)
    load_w.wait()

    def widen(c):
        for kk in range(2):
            for part, wide in enumerate((w2r, w2i)):
                block = w[kk, part, c].astype(F32)
                wide[kk, c] = jnp.concatenate([block, block], axis=1)

    loop(0, C, widen)
    load_rows.wait()
    loop(0, NI, lambda i: to_modes(0, i))

    def pointwise(n):
        start = pl.multiple_of(n * CHUNK, CHUNK)
        mine = expand_matrix(start)
        rows_of = dot(mine, lw_ref[...], 1, 1).astype(BF)
        for i, block in mix_rows(rows_of):
            kron[:, i * CHUNK : (i + 1) * CHUNK] = block
        offset = jnp.sum(mine.astype(F32) * bias_ref[...], axis=1, keepdims=True)
        pre[pl.ds(start, CHUNK)] = dot(kron[...], x[...]) + offset

    loop(0, NI, pointwise)
    to_owners(0)

    def turn(rnd):
        for m in range(2):
            rows_of = c_in[rnd, m].reshape(128, KH)
            turned[m] = (pltpu.roll(rows_of, 64, 1) * half_sign()).reshape(NQ, 8, KH)

    wait(c_in.at[0], rc.at[0])
    turn(0)
    for kk in range(2):

        def mix(qq, sums):
            sums = list(sums)
            for i in range(NI):
                real = w2r[kk, 16 * i + qq]
                imag = w2i[kk, 16 * i + qq]
                for m in range(2):
                    row = 2 * i + kk
                    sums[m] = sums[m] + c_in[0, m, qq, row : row + 1] * real + turned[m, qq, row : row + 1] * imag
            return tuple(sums)

        sums = lax.fori_loop(0, NQ, mix, (jnp.zeros((C, KH), F32),) * 2)
        for m in range(2):
            mixed[m, kk * C : (kk + 1) * C] = sums[m]
    copy_xm = pltpu.make_async_copy(c_in.at[0], xm_hbm, store.at[NI])
    copy_xm.start()
    from_owners(0)

    load_t1t.wait()
    load_cot.wait()

    def second(i):
        start = pl.multiple_of(i * CHUNK, CHUNK)
        part = pl.ds(start, CHUNK)
        wait(f_in.at[0, i], rf.at[0, i])
        pre[part] += dot(f_in[0, i].reshape(CHUNK, 2 * KW), t1t[...])

        def slab(s):
            at = pl.ds(pl.multiple_of(start + s * 16, 16), 16)
            slopes[at] = (cot[at].astype(F32) * gelu_slope(pre[at])).astype(BF)

        loop(0, CHUNK // 16, slab)
        pltpu.make_async_copy(slopes.at[part], slopes_hbm.at[part], store.at[i]).start()
        scale = jnp.concatenate([column_scale()] * 2, axis=1)
        a_out[1, i] = (dot(slopes[part], t1[...]) * scale).astype(BF).reshape(NQ, R, 2 * KW)
        send_plane(a_out, a_in, sa, ra, 1, i)

    loop(0, NI, second)
    loop(0, NI, lambda i: to_modes(1, i))
    to_owners(1)
    wait(c_in.at[1], rc.at[1])
    for m in range(2):
        nat[m] = dot(natural_ref[...], c_in[1, m].reshape(128, KH).astype(BF))
        turned[m] = (pltpu.roll(nat[m], 64, 1) * -half_sign()).reshape(NQ, 8, KH)
    copy_gm = pltpu.make_async_copy(nat, gm_hbm, store.at[NI + 1])
    copy_gm.start()
    for kk in range(2):
        at = slice(kk * C, (kk + 1) * C)
        grads = [nat[m, at] for m in range(2)]
        grads_turned = [turned[m].reshape(128, KH)[at] for m in range(2)]

        def mix_back(c8):
            rows_of = ([], [])
            for n in range(8):
                c = c8 * 8 + n
                real = w2r[kk, c]
                imag = w2i[kk, c]
                for m in range(2):
                    rows_of[m].append(jnp.sum(grads[m] * real + grads_turned[m] * imag, axis=0, keepdims=True))
            for m in range(2):
                mixed[m, pl.ds(pl.multiple_of(kk * C + c8 * 8, 8), 8)] = jnp.concatenate(rows_of[m], axis=0)

        loop(0, C // 8, mix_back)
    from_owners(1)

    def last(i):
        wait(f_in.at[1, i], rf.at[1, i])
        part = pl.ds(pl.multiple_of(i * NQ, NQ), NQ)
        pltpu.make_async_copy(f_in.at[1, i], back_hbm.at[part], store.at[NI + 2 + i]).start()

    loop(0, NI, last)

    for i in range(NI):
        part = pl.ds(i * CHUNK, CHUNK)
        pltpu.make_async_copy(slopes.at[part], slopes_hbm.at[part], store.at[i]).wait()
        pltpu.make_async_copy(f_in.at[1, i], back_hbm.at[pl.ds(i * NQ, NQ)], store.at[NI + 2 + i]).wait()
    copy_xm.wait()
    copy_gm.wait()
    for rnd in range(2):
        for i in range(NI):
            wait(a_out.at[rnd, i, pl.ds(0, NQ - 1)], sa.at[rnd, i])
            wait(f_out.at[rnd, i, pl.ds(0, NQ - 1)], sf.at[rnd, i])
            wait(b_out.at[rnd, i, pl.ds(0, NZ - 1)], sb.at[rnd, i])
            wait(e_in.at[rnd, i, pl.ds(0, NZ - 1)], se.at[rnd, i])
        for out, s in ((c_out, sc), (d_out, sd)):
            wait(out.at[rnd, 0, pl.ds(0, NQ - 1)], s.at[rnd, 0])
            wait(out.at[rnd, 0], s.at[rnd, 1])


def outputs(
    slopes, back, t1t, lw, xm, gm, sg_hbm, wg_hbm,
    kron, sg, wg, xr, xi, turned, store_s, store_w,
):
    for m in range(2):
        rows_of = xm[m].reshape(128, KH)
        swapped = pltpu.roll(rows_of, 64, 1)
        low = lax.broadcasted_iota(jnp.int32, (128, KH), 1) < 64
        xr[m] = jnp.where(low, rows_of, swapped).reshape(NQ, 8, KH)
        xi[m] = jnp.where(low, swapped, rows_of).reshape(NQ, 8, KH)
        turned[m] = pltpu.roll(gm[m], 64, 1) * -half_sign()
    for kk in range(2):
        at = slice(kk * C, (kk + 1) * C)
        for i in range(NI):

            def term(qq, carry):
                row = 2 * i + kk
                total = jnp.zeros((C, KH), F32)
                for m in range(2):
                    total = total + xr[m, qq, row : row + 1] * gm[m, at] + xi[m, qq, row : row + 1] * turned[m, at]
                wg[kk, 0, 16 * i + qq] = total[:, :64]
                wg[kk, 1, 16 * i + qq] = total[:, 64:]
                return carry

            lax.fori_loop(0, NQ, term, 0)
        pltpu.make_async_copy(wg.at[kk], wg_hbm.at[kk], store_w.at[kk]).start()

    def surface_part(n, carry):
        start = pl.multiple_of(n * CHUNK, CHUNK)
        rows_of = dot(expand_matrix(start), lw[...]).astype(BF)
        for i, block in mix_rows(rows_of):
            kron[:, i * CHUNK : (i + 1) * CHUNK] = block
        part = pl.ds(start, CHUNK)
        sg[part] = (dot(kron[...], slopes[...]) + dot(back[part], t1t[...])).astype(BF)
        pltpu.make_async_copy(sg.at[part], sg_hbm.at[part], store_s.at[n]).start()
        return carry

    lax.fori_loop(0, NI, surface_part, 0)
    for n in range(NI):
        part = pl.ds(n * CHUNK, CHUNK)
        pltpu.make_async_copy(sg.at[part], sg_hbm.at[part], store_s.at[n]).wait()
    for kk in range(2):
        pltpu.make_async_copy(wg.at[kk], wg_hbm.at[kk], store_w.at[kk]).wait()


def local(surface, cotangent, spectral_weight, local_weight, bias_vector):
    columns, rows = tables()
    t1 = jnp.asarray(columns, BF)
    t1t = jnp.asarray(columns.T, BF)
    row_table = jnp.asarray(rows, BF)
    gather, spread, modes, natural = (jnp.asarray(p, BF) for p in permutations())
    anywhere = pl.BlockSpec(memory_space=pl.ANY)
    vmem = pl.BlockSpec(memory_space=pltpu.VMEM)
    DMA = pltpu.SemaphoreType.DMA
    V = pltpu.VMEM
    shape = jax.ShapeDtypeStruct
    slopes, back, xm, gm = pl.pallas_call(
        transfers,
        out_shape=(
            shape((ROWS, W), BF),
            shape((C, R, 2 * KW), BF),
            shape((2, NQ, 8, KH), F32),
            shape((2, 128, KH), F32),
        ),
        in_specs=[anywhere] * 6 + [vmem] * 6,
        out_specs=[anywhere] * 4,
        scratch_shapes=[
            V((ROWS, W), BF),
            V((ROWS, W), BF),
            V((2, 2, C, C, 64), BF),
            V((W, 2 * KW), BF),
            V((2 * KW, W), BF),
            V((2 * CHUNK, 2 * KH), BF),
            V((2, C, C, KH), F32),
            V((2, C, C, KH), F32),
            V((CHUNK, ROWS), BF),
            V((ROWS, W), F32),
            V((ROWS, W), BF),
            V((2, NI, NQ, R, 2 * KW), BF),
            V((2, NI, NQ, R, 2 * KW), BF),
            V((2, NI, NZ, 32, 2 * KH), BF),
            V((2, NI, NZ, 32, 2 * KH), BF),
            V((2, 2, NQ, 8, KH), F32),
            V((2, 2, NQ, 8, KH), F32),
            V((2, 2, NQ, 8, KH), F32),
            V((2, 2, NQ, 8, KH), F32),
            V((2, NI, 32, 2 * KH), BF),
            V((2, NI, NZ, 32, 2 * KH), BF),
            V((2, NI, NQ, R, 2 * KW), BF),
            V((2, NI, NQ, R, 2 * KW), BF),
            V((2, NQ, 8, KH), F32),
            V((2, 128, KH), F32),
            V((2, 128, KH), F32),
            DMA((9,)),
            DMA((NI + 2 + NI,)),
            DMA((2, NI)),
            DMA((2, NI)),
            DMA((2, NI)),
            DMA((2,)),
            DMA((2, 2)),
            DMA((2,)),
            DMA((2, 2)),
            DMA((2,)),
            DMA((2, NI)),
            DMA((2, NI)),
            DMA((2, NI)),
            DMA((2, NI)),
        ],
        compiler_params=pltpu.CompilerParams(
            collective_id=0, has_side_effects=True, vmem_limit_bytes=56 * 1024 * 1024
        ),
        name="transfers",
    )(
        surface.reshape(ROWS, W),
        cotangent.reshape(ROWS, W),
        spectral_weight,
        t1,
        t1t,
        row_table,
        local_weight,
        bias_vector.reshape(1, C),
        gather,
        spread,
        modes,
        natural,
    )
    surface_gradient, weight_gradient = pl.pallas_call(
        outputs,
        out_shape=(shape((ROWS, W), BF), shape((2, 2, C, C, 64), F32)),
        in_specs=[vmem] * 6,
        out_specs=[anywhere] * 2,
        scratch_shapes=[
            V((CHUNK, ROWS), BF),
            V((ROWS, W), BF),
            V((2, 2, C, C, 64), F32),
            V((2, NQ, 8, KH), F32),
            V((2, NQ, 8, KH), F32),
            V((2, 128, KH), F32),
            DMA((NI,)),
            DMA((2,)),
        ],
        compiler_params=pltpu.CompilerParams(vmem_limit_bytes=48 * 1024 * 1024),
        name="outputs",
    )(slopes, back.reshape(ROWS, 2 * KW), t1t, local_weight, xm, gm)
    return surface_gradient.reshape(1, C, R, W), weight_gradient


def solution(mesh):
    placed = (
        P("batch", None, "rows", None),
        P("batch", None, "rows", None),
        P("rows", None, None, None, "batch"),
        P(),
        P(),
    )
    return jax.shard_map(
        local,
        mesh=mesh,
        in_specs=placed,
        out_specs=(P("batch", None, "rows", None), P("rows", None, None, None, "batch")),
        check_vma=False,
    )
```

profile of v0, /device:TPU:1, one launch (start us, length us, event | category | flops | bytes accessed | tf_op | source)
XLA Modules:
  0.0 143.6 jit_solution(1298565100744783212)
XLA Ops:
  0.6 0.0 copy-start
  0.6 0.0 copy-start.5
  0.7 121.7 %transfers.1 = (bf16[1024,1024]{1,0:T(8,128)(2,1)}, bf16[64,16,512]{2,1,0:T(8,128)(2,1)}, f32[2,16,8,128]{3,2,1,0:T(8,128)}, f32[2,128,128]{2,1,0:T(8,128)}) custom-call(bf16[1024,1024]{1,0:T(8,128)(2,1)} %bitcast.6, bf16[1024,1024]{1,0:T(8,128)(2,1)} %bitcast.7, bf16[2,2,64,64,64]{4,3,2,1,0:T(8,128)(2,1)} %w_hbm.1, ...), custom_call_target="tpu_custom_call" | custom-call | tf_op jit(solution)/shard_map/transfers/pallas_call | solution.py:419
  122.4 0.0 copy-done
  122.4 0.0 copy-done.5
  122.4 0.0 copy-start.1
  122.4 1.6 %copy-done.1 = bf16[1024,1024]{1,0:T(8,128)(2,1)S(1)} copy-done((bf16[1024,1024]{1,0:T(8,128)(2,1)S(1)}, bf16[1024,1024]{1,0:T(8,128)(2,1)}, u32[]{:S(2)}) %copy-start.1) | copy-done | bytes 2097176
  124.0 0.0 copy-start.2
  124.0 1.2 copy-done.2
  125.2 0.0 copy-start.3
  125.2 0.9 copy-done.3
  126.1 0.0 copy-start.4
  126.1 0.9 copy-done.4
  127.0 16.6 %outputs.1 = (bf16[1024,1024]{1,0:T(8,128)(2,1)}, f32[2,2,64,64,64]{4,3,2,1,0:T(8,128)}) custom-call(bf16[1024,1024]{1,0:T(8,128)(2,1)S(1)} %copy-done.1, bf16[1024,512]{1,0:T(8,128)(2,1)S(1)} %bitcast.5, bf16[512,1024]{1,0:T(8,128)(2,1)S(1)} %copy-done, bf16[64,64]{1,0:T(8,128)(2,1)S(1)} %copy-done.5, f32[2,16,8,128]{3,2,1,0:T(8,128)S(1)} %copy-done.3, ...), custom_call_target="tpu_custom_call" | custom-call | tf_op jit(solution)/shard_map/outputs/pallas_call | solution.py:489
Async XLA Ops:
  0.6 121.8 %copy-start = (bf16[512,1024]{1,0:T(8,128)(2,1)S(1)}, bf16[512,1024]{1,0:T(8,128)(2,1)}, u32[]{:S(2)}) copy-start(bf16[512,1024]{1,0:T(8,128)(2,1)} %constant.15.clone.t1t_hbm.t1t) | copy-start | bytes 3145732
  0.6 121.8 %copy-start.5 = (bf16[64,64]{1,0:T(8,128)(2,1)S(1)}, bf16[64,64]{1,0:T(8,128)(2,1)}, u32[]{:S(2)}) copy-start(bf16[64,64]{1,0:T(8,128)(2,1)} %lw.1) | copy-start | bytes 24580
  122.4 1.6 %copy-start.1 = (bf16[1024,1024]{1,0:T(8,128)(2,1)S(1)}, bf16[1024,1024]{1,0:T(8,128)(2,1)}, u32[]{:S(2)}) copy-start(bf16[1024,1024]{1,0:T(8,128)(2,1)} %get-tuple-element.8.slopes) | copy-start | bytes 6291460
  124.0 1.2 copy-start.2
  125.2 0.9 copy-start.3
  126.1 0.9 copy-start.4
where the time goes:
time: 144 us
  Pallas kernels  138 us (96%)
  local copies, waits for them, and re-layouts  4.63 us (3%)
    pallas_call x1, Pallas kernels, local(): pl.pallas_call(transfers, out_shape=(shape((ROWS, W), BF), shape((C, R, 2...  122 us
    pallas_call x1, Pallas kernels, local(): pl.pallas_call(outputs, out_shape=(shape((ROWS, W), BF), shape((2, 2, C,...  16.6 us
    unnamed x12, local copies, waits for them, and re-layouts  4.63 us

commit v1 on v0

v1 whole, which is shorter than its diff:
```python
import math

import jax
import jax.numpy as jnp
import numpy as np
from jax import lax
from jax.experimental import pallas as pl
from jax.experimental.pallas import tpu as pltpu
from jax.sharding import PartitionSpec as P

MESH = pl.DeviceIdType.MESH
BF = jnp.bfloat16
F32 = jnp.float32

C = 64
R = 16
W = 1024
KW = 256
KO = KW // 2
KH = 128
NZ = 8
NQ = 16
NI = 4
ROWS = C * R
CHUNK = NQ * R


def tables():
    w = np.arange(W)[:, None]
    columns = []
    for kk in range(2):
        k = 2 * np.arange(KO)[None, :] + kk
        angle = 2 * np.pi * ((w * k) % W) / W
        columns += [np.cos(angle), -np.sin(angle)]
    columns = np.concatenate(columns, axis=1)
    height = NZ * NQ * R
    jj = np.arange(KH // 2)
    rows = np.zeros((NZ, 2 * CHUNK, 2 * KH))
    for z in range(NZ):
        h = (z * CHUNK + np.arange(CHUNK))[:, None]
        for half in range(2):
            f = (jj - half * (KH // 2))[None, :]
            angle = 2 * np.pi * ((f * h) % height) / height
            cos, sin = np.cos(angle), np.sin(angle)
            at = half * KH
            rows[z, :CHUNK, at : at + 64] = cos
            rows[z, :CHUNK, at + 64 : at + 128] = -sin
            rows[z, CHUNK:, at : at + 64] = sin
            rows[z, CHUNK:, at + 64 : at + 128] = cos
    return columns, rows


def permutations():
    gather = np.zeros((NQ, NI, NI, NZ, NQ))
    spread = np.zeros((NQ, NI, C))
    for q in range(NQ):
        for i in range(NI):
            gather[q, i, i, :, q] = 1
            spread[q, i, 16 * i + q] = 1
    gather = gather.reshape(64, 512)
    spread = spread.reshape(64, 64)
    return gather, spread, spread.T.copy()


def dot(a, b, ca=1, cb=0):
    return lax.dot_general(a, b, (((ca,), (cb,)), ((), ())), preferred_element_type=F32)


def gelu_slope(v):
    cumulative = 0.5 * (1.0 + lax.erf(v * (1.0 / math.sqrt(2.0))))
    density = jnp.exp(-0.5 * v * v) * (1.0 / math.sqrt(2.0 * math.pi))
    return cumulative + v * density


def expand_matrix(start):
    row = lax.broadcasted_iota(jnp.int32, (CHUNK, C), 0) + start
    col = lax.broadcasted_iota(jnp.int32, (CHUNK, C), 1)
    return (row // R == col).astype(F32).astype(BF)


def same_row_mask():
    row = lax.broadcasted_iota(jnp.int32, (CHUNK, CHUNK), 0) % R
    col = lax.broadcasted_iota(jnp.int32, (CHUNK, CHUNK), 1) % R
    return row == col


def mix_rows(weight_rows):
    mask = same_row_mask()
    for i in range(NI):
        spread = dot(weight_rows, expand_matrix(i * CHUNK), 1, 1)
        yield i, jnp.where(mask, spread, 0.0).astype(BF)


def column_scale(kk):
    if kk:
        return jnp.full((1, 2 * KO), 2.0**-20, F32)
    lane = lax.broadcasted_iota(jnp.int32, (1, 2 * KO), 1)
    return jnp.where(lane % KO == 0, 2.0**-21, 2.0**-20).astype(F32)


def half_sign():
    lane = lax.broadcasted_iota(jnp.int32, (1, 128), 1)
    return jnp.where(lane < 64, -1.0, 1.0).astype(F32)


def transfers(
    x_hbm, cot_hbm, w_hbm, t1_hbm, t1t_hbm, rows_hbm, lw_ref, bias_ref, gather_ref, spread_ref, natural_ref,
    sg_hbm, xm_hbm, gm_hbm,
    x, cot, w, t1, t1t, rt, w2r, w2i, kron, pre, slopes,
    a_out, a_in, b_out, b_in, c_out, c_in, d_out, d_in, e_out, e_in, f_out, f_in, turned, mixed, nat,
    load, store, sa, ra, sb, rb, sc, rc, sd, rd, se, re, sf, rf,
):
    b = lax.axis_index("batch")
    d = lax.axis_index("rows")
    z = d // NQ
    q = d % NQ

    def in_plane(p):
        return lax.rem(q + p, NQ)

    def along(p):
        return lax.rem(z + p, NZ)

    def wait(ref, sem):
        pltpu.make_async_copy(ref, ref, sem).wait()

    def send(src, dst, s, r, batch, row):
        pltpu.make_async_remote_copy(
            src_ref=src, dst_ref=dst, send_sem=s, recv_sem=r, device_id=(batch, row), device_id_type=MESH
        ).start()

    def loop(lo, hi, body):
        def step(p, carry):
            body(p)
            return carry

        lax.fori_loop(lo, hi, step, 0)

    barrier = pltpu.get_barrier_semaphore()

    def greet(batch, row):
        pl.semaphore_signal(barrier, inc=1, device_id=(batch, row), device_id_type=MESH)

    loads = []
    for i in range(NI):
        part = pl.ds(i * CHUNK, CHUNK)
        loads.append(pltpu.make_async_copy(x_hbm.at[part], x.at[part], load.at[i]))
    load_t1 = pltpu.make_async_copy(t1_hbm, t1, load.at[4])
    load_rows = pltpu.make_async_copy(rows_hbm.at[z], rt, load.at[5])
    load_w = pltpu.make_async_copy(w_hbm, w, load.at[6])
    load_t1t = pltpu.make_async_copy(t1t_hbm, t1t, load.at[7])
    load_cot = pltpu.make_async_copy(cot_hbm, cot, load.at[8])
    load_t1.start()
    for copy in loads:
        copy.start()
    loop(1, NQ, lambda p: greet(b, z * NQ + in_plane(p)))
    loop(0, NQ, lambda p: greet(1 - b, z * NQ + p))
    loop(1, NZ, lambda p: greet(b, along(p) * NQ + q))
    for copy in (load_rows, load_w, load_t1t, load_cot):
        copy.start()

    def split_columns(rnd, i, rows_of):
        field = dot(rows_of, t1[...])
        for kk in range(2):
            half = field[:, kk * 256 : (kk + 1) * 256]
            if rnd:
                half = half * column_scale(kk)
            a_out[rnd, kk, i] = half.astype(BF).reshape(NQ, R, 256)

    load_t1.wait()

    def first(i):
        part = pl.ds(pl.multiple_of(i * CHUNK, CHUNK), CHUNK)
        pltpu.make_async_copy(x_hbm.at[part], x.at[part], load.at[i]).wait()
        split_columns(0, i, x[part])

    loop(0, NI, first)
    pl.semaphore_wait(barrier, 2 * NQ - 1 + NZ - 1)

    def send_plane(out, into, s, r, rnd, kk, i):
        def one(p):
            to = in_plane(p)
            send(
                out.at[rnd, kk, i, to], into.at[rnd, kk, i, q], s.at[rnd, kk, i], r.at[rnd, kk, i], b, z * NQ + to
            )

        loop(1, NQ, one)
        pltpu.make_async_copy(out.at[rnd, kk, i, q], into.at[rnd, kk, i, q], r.at[rnd, kk, i]).start()

    def sent_plane(out, s, rnd, kk, i):
        wait(out.at[rnd, kk, i, pl.ds(0, NQ - 1)], s.at[rnd, kk, i])

    def send_owners(out, into, s, r, rnd, kk):
        def same(p):
            to = in_plane(p)
            send(
                out.at[rnd, kk, b, to], into.at[rnd, kk, b, q], s.at[rnd, kk, 0], r.at[rnd, kk], b, z * NQ + to
            )

        def other(p):
            to = in_plane(p)
            send(
                out.at[rnd, kk, 1 - b, to], into.at[rnd, kk, b, q], s.at[rnd, kk, 1], r.at[rnd, kk], 1 - b, z * NQ + to
            )

        loop(0, NQ, other)
        loop(1, NQ, same)
        pltpu.make_async_copy(out.at[rnd, kk, b, q], into.at[rnd, kk, b, q], r.at[rnd, kk]).start()

    def to_modes(rnd, kk):
        def one_channel(i):
            wait(a_in.at[rnd, kk, i], ra.at[rnd, kk, i])
            plane = a_in[rnd, kk, i].reshape(CHUNK, 2 * KO)
            term = dot(plane[:, :KO], rt[:CHUNK], 0, 0) + dot(plane[:, KO:], rt[CHUNK:], 0, 0)
            b_out[rnd, kk, i] = term.astype(BF).reshape(NZ, NQ, 2 * KH)

            def one(p):
                to = along(p)
                send(
                    b_out.at[rnd, kk, i, to], b_in.at[rnd, kk, i, z], sb.at[rnd, kk, i], rb.at[rnd, kk], b, to * NQ + q
                )

            loop(1, NZ, one)
            pltpu.make_async_copy(b_out.at[rnd, kk, i, z], b_in.at[rnd, kk, i, z], rb.at[rnd, kk]).start()

        loop(0, NI, one_channel)

    def to_owners(rnd, kk):
        wait(b_in.at[rnd, kk], rb.at[rnd, kk])
        total = dot(gather_ref[...], b_in[rnd, kk].reshape(512, 2 * KH))
        for half in range(2):
            c_out[rnd, kk, half] = total[:, half * KH : (half + 1) * KH].reshape(NQ, NI, KH)
        send_owners(c_out, c_in, sc, rc, rnd, kk)

    def from_owners(rnd, kk):
        for m in range(2):
            d_out[rnd, kk, m] = dot(spread_ref[...], mixed[m].astype(BF)).reshape(NQ, NI, KH)
        send_owners(d_out, d_in, sd, rd, rnd, kk)

    def spread_modes(rnd, kk):
        wait(d_in.at[rnd, kk], rd.at[rnd, kk])
        halves = [dot(natural_ref[...], d_in[rnd, kk, half].reshape(C, KH).astype(BF)) for half in range(2)]
        e_out[rnd, kk] = jnp.concatenate(halves, axis=1).astype(BF).reshape(NI, NQ, 2 * KH)

        def one_channel(i):
            def one(p):
                to = along(p)
                send(e_out.at[rnd, kk, i], e_in.at[rnd, kk, i, z], se.at[rnd, kk, i], re.at[rnd, kk, i], b, to * NQ + q)

            loop(1, NZ, one)
            pltpu.make_async_copy(e_out.at[rnd, kk, i], e_in.at[rnd, kk, i, z], re.at[rnd, kk, i]).start()

        loop(0, NI, one_channel)

    def to_rows(rnd, kk, lo=0, hi=NI):
        def one_channel(i):
            wait(e_in.at[rnd, kk, i], re.at[rnd, kk, i])
            both = dot(rt[...], e_in[rnd, kk, i].reshape(KO, 2 * KH), 1, 1)
            both = jnp.concatenate([both[:CHUNK], both[CHUNK:]], axis=1)
            if rnd == 0:
                both = both * column_scale(kk)
            f_out[rnd, kk, i] = both.astype(BF).reshape(NQ, R, 2 * KO)
            send_plane(f_out, f_in, sf, rf, rnd, kk, i)

        loop(lo, hi, one_channel)

    def from_rows(rnd, i):
        start = pl.multiple_of(i * CHUNK, CHUNK)
        total = pre[pl.ds(start, CHUNK)]
        for kk in range(2):
            wait(f_in.at[rnd, kk, i], rf.at[rnd, kk, i])
            total = total + dot(f_in[rnd, kk, i].reshape(CHUNK, 2 * KO), t1t[kk * 256 : (kk + 1) * 256])
        return total

    def pointwise(rnd, lo, hi):
        field, over = ((x, 1), (slopes, 0))[rnd]

        def rows_of_one(n):
            start = pl.multiple_of(n * CHUNK, CHUNK)
            mine = expand_matrix(start)
            for i, block in mix_rows(dot(mine, lw_ref[...], 1, over).astype(BF)):
                kron[:, i * CHUNK : (i + 1) * CHUNK] = block
            part = pl.ds(start, CHUNK)
            pre[part] = dot(kron[...], field[...])
            if rnd == 0:
                pre[part] += jnp.sum(mine.astype(F32) * bias_ref[...], axis=1, keepdims=True)

        loop(lo, hi, rows_of_one)

    def widen(c):
        for kk in range(2):
            for part, wide in enumerate((w2r, w2i)):
                block = w[kk, part, c].astype(F32)
                wide[kk, c] = jnp.concatenate([block, block], axis=1)

    def mix(kk):
        wait(c_in.at[0, kk], rc.at[0, kk])
        for m in range(2):
            rows_of = c_in[0, kk, m].reshape(C, KH)
            turned[m] = (pltpu.roll(rows_of, 64, 1) * half_sign()).reshape(NQ, NI, KH)

        def terms(qq, sums):
            sums = list(sums)
            for i in range(NI):
                real = w2r[kk, 16 * i + qq]
                imag = w2i[kk, 16 * i + qq]
                for m in range(2):
                    sums[m] = sums[m] + c_in[0, kk, m, qq, i : i + 1] * real + turned[m, qq, i : i + 1] * imag
            return tuple(sums)

        sums = lax.fori_loop(0, NQ, terms, (jnp.zeros((C, KH), F32),) * 2)
        for m in range(2):
            mixed[m] = sums[m]

    def mix_back(kk):
        wait(c_in.at[1, kk], rc.at[1, kk])
        grads = []
        grads_turned = []
        for m in range(2):
            grads.append(dot(natural_ref[...], c_in[1, kk, m].reshape(C, KH).astype(BF)))
            grads_turned.append(pltpu.roll(grads[m], 64, 1) * -half_sign())
            nat[kk, m] = grads[m]

        def terms(c8):
            rows_of = ([], [])
            for n in range(8):
                c = c8 * 8 + n
                real = w2r[kk, c]
                imag = w2i[kk, c]
                for m in range(2):
                    rows_of[m].append(jnp.sum(grads[m] * real + grads_turned[m] * imag, axis=0, keepdims=True))
            for m in range(2):
                mixed[m, pl.ds(pl.multiple_of(c8 * 8, 8), 8)] = jnp.concatenate(rows_of[m], axis=0)

        loop(0, C // 8, terms)

    for i in range(NI):
        send_plane(a_out, a_in, sa, ra, 0, 0, i)
    load_w.wait()
    loop(0, 24, widen)
    for i in range(NI):
        sent_plane(a_out, sa, 0, 0, i)
        send_plane(a_out, a_in, sa, ra, 0, 1, i)
        if i < 2:
            pointwise(0, i, i + 1)
    load_rows.wait()
    to_modes(0, 0)
    loop(24, 40, widen)
    to_modes(0, 1)
    to_owners(0, 0)
    loop(40, C, widen)
    to_owners(0, 1)
    mix(0)
    from_owners(0, 0)
    pointwise(0, 2, 3)
    mix(1)
    from_owners(0, 1)
    pointwise(0, 3, 4)
    spread_modes(0, 0)
    to_rows(0, 0, 0, 2)
    spread_modes(0, 1)
    to_rows(0, 0, 2, 4)
    to_rows(0, 1)
    copy_xm = pltpu.make_async_copy(c_in.at[0], xm_hbm, store.at[NI])
    copy_xm.start()

    load_t1t.wait()
    load_cot.wait()

    def second(i):
        start = pl.multiple_of(i * CHUNK, CHUNK)
        part = pl.ds(start, CHUNK)
        pre[part] = from_rows(0, i)

        def slab(s):
            at = pl.ds(pl.multiple_of(start + s * 16, 16), 16)
            slopes[at] = (cot[at].astype(F32) * gelu_slope(pre[at])).astype(BF)

        loop(0, CHUNK // 16, slab)
        split_columns(1, i, slopes[part])
        send_plane(a_out, a_in, sa, ra, 1, 0, i)

    loop(0, NI, second)
    for i in range(NI):
        send_plane(a_out, a_in, sa, ra, 1, 1, i)
    to_modes(1, 0)
    to_modes(1, 1)
    to_owners(1, 0)
    pointwise(1, 0, 2)
    to_owners(1, 1)
    mix_back(0)
    from_owners(1, 0)
    pointwise(1, 2, 3)
    mix_back(1)
    from_owners(1, 1)
    pointwise(1, 3, 4)
    spread_modes(1, 0)
    to_rows(1, 0, 0, 2)
    spread_modes(1, 1)
    to_rows(1, 0, 2, 4)
    to_rows(1, 1)
    copy_gm = pltpu.make_async_copy(nat, gm_hbm, store.at[NI + 1])
    copy_gm.start()

    def last(i):
        part = pl.ds(pl.multiple_of(i * CHUNK, CHUNK), CHUNK)
        x[part] = from_rows(1, i).astype(BF)
        pltpu.make_async_copy(x.at[part], sg_hbm.at[part], store.at[i]).start()

    loop(0, NI, last)

    for i in range(NI):
        part = pl.ds(i * CHUNK, CHUNK)
        pltpu.make_async_copy(x.at[part], sg_hbm.at[part], store.at[i]).wait()
    copy_xm.wait()
    copy_gm.wait()
    for rnd in range(2):
        for kk in range(2):

            def ended(i):
                sent_plane(f_out, sf, rnd, kk, i)
                wait(b_out.at[rnd, kk, i, pl.ds(0, NZ - 1)], sb.at[rnd, kk, i])
                wait(e_in.at[rnd, kk, i, pl.ds(0, NZ - 1)], se.at[rnd, kk, i])
                if rnd or kk:
                    sent_plane(a_out, sa, rnd, kk, i)

            loop(0, NI, ended)
            for out, s in ((c_out, sc), (d_out, sd)):
                wait(out.at[rnd, kk, 0, pl.ds(0, NQ - 1)], s.at[rnd, kk, 0])
                wait(out.at[rnd, kk, 0], s.at[rnd, kk, 1])


def outputs(sg_in, xm, gm, sg_hbm, wg_hbm, sg, wg, xr, xi, turned, load, store_s, store_w):
    loads, passes = [], []
    for n in range(NI):
        part = pl.ds(n * CHUNK, CHUNK)
        loads.append(pltpu.make_async_copy(sg_in.at[part], sg.at[part], load.at[n]))
        passes.append(pltpu.make_async_copy(sg.at[part], sg_hbm.at[part], store_s.at[n]))
        loads[n].start()
    low = lax.broadcasted_iota(jnp.int32, (C, KH), 1) < 64
    stores = []
    for kk in range(2):
        for m in range(2):
            rows_of = xm[kk, m].reshape(C, KH)
            swapped = pltpu.roll(rows_of, 64, 1)
            xr[m] = jnp.where(low, rows_of, swapped).reshape(NQ, NI, KH)
            xi[m] = jnp.where(low, swapped, rows_of).reshape(NQ, NI, KH)
            turned[m] = pltpu.roll(gm[kk, m], 64, 1) * -half_sign()
        for i in range(NI):

            def terms(q4, carry):
                for n in range(4):
                    qq = q4 * 4 + n
                    total = jnp.zeros((C, KH), F32)
                    for m in range(2):
                        total = total + xr[m, qq, i : i + 1] * gm[kk, m] + xi[m, qq, i : i + 1] * turned[m]
                    wg[kk, 0, 16 * i + qq] = total[:, :64]
                    wg[kk, 1, 16 * i + qq] = total[:, 64:]
                return carry

            lax.fori_loop(0, NQ // 4, terms, 0)
            for part in range(2):
                block = (kk, part, pl.ds(16 * i, 16))
                stores.append(pltpu.make_async_copy(wg.at[block], wg_hbm.at[block], store_w.at[kk, part, i]))
                stores[-1].start()
            if kk == 0:
                loads[i].wait()
                passes[i].start()
    for store in stores + passes:
        store.wait()


def local(surface, cotangent, spectral_weight, local_weight, bias_vector):
    columns, rows = tables()
    t1 = jnp.asarray(columns, BF)
    t1t = jnp.asarray(columns.T, BF)
    row_table = jnp.asarray(rows, BF)
    gather, spread, natural = (jnp.asarray(p, BF) for p in permutations())
    anywhere = pl.BlockSpec(memory_space=pl.ANY)
    vmem = pl.BlockSpec(memory_space=pltpu.VMEM)
    DMA = pltpu.SemaphoreType.DMA
    V = pltpu.VMEM
    shape = jax.ShapeDtypeStruct
    surface_gradient, xm, gm = pl.pallas_call(
        transfers,
        out_shape=(
            shape((ROWS, W), BF),
            shape((2, 2, NQ, NI, KH), F32),
            shape((2, 2, C, KH), F32),
        ),
        in_specs=[anywhere] * 6 + [vmem] * 5,
        out_specs=[anywhere] * 3,
        scratch_shapes=[
            V((ROWS, W), BF),
            V((ROWS, W), BF),
            V((2, 2, C, C, 64), BF),
            V((W, 2 * KW), BF),
            V((2 * KW, W), BF),
            V((2 * CHUNK, 2 * KH), BF),
            V((2, C, C, KH), F32),
            V((2, C, C, KH), F32),
            V((CHUNK, ROWS), BF),
            V((ROWS, W), F32),
            V((ROWS, W), BF),
            V((2, 2, NI, NQ, R, 2 * KO), BF),
            V((2, 2, NI, NQ, R, 2 * KO), BF),
            V((2, 2, NI, NZ, NQ, 2 * KH), BF),
            V((2, 2, NI, NZ, NQ, 2 * KH), BF),
            V((2, 2, 2, NQ, NI, KH), F32),
            V((2, 2, 2, NQ, NI, KH), F32),
            V((2, 2, 2, NQ, NI, KH), F32),
            V((2, 2, 2, NQ, NI, KH), F32),
            V((2, 2, NI, NQ, 2 * KH), BF),
            V((2, 2, NI, NZ, NQ, 2 * KH), BF),
            V((2, 2, NI, NQ, R, 2 * KO), BF),
            V((2, 2, NI, NQ, R, 2 * KO), BF),
            V((2, NQ, NI, KH), F32),
            V((2, C, KH), F32),
            V((2, 2, C, KH), F32),
            DMA((9,)),
            DMA((NI + 2,)),
            DMA((2, 2, NI)),
            DMA((2, 2, NI)),
            DMA((2, 2, NI)),
            DMA((2, 2)),
            DMA((2, 2, 2)),
            DMA((2, 2)),
            DMA((2, 2, 2)),
            DMA((2, 2)),
            DMA((2, 2, NI)),
            DMA((2, 2, NI)),
            DMA((2, 2, NI)),
            DMA((2, 2, NI)),
        ],
        compiler_params=pltpu.CompilerParams(
            collective_id=0, has_side_effects=True, vmem_limit_bytes=56 * 1024 * 1024
        ),
        name="transfers",
    )(
        surface.reshape(ROWS, W),
        cotangent.reshape(ROWS, W),
        spectral_weight,
        t1,
        t1t,
        row_table,
        local_weight,
        bias_vector.reshape(1, C),
        gather,
        spread,
        natural,
    )
    surface_gradient, weight_gradient = pl.pallas_call(
        outputs,
        out_shape=(shape((ROWS, W), BF), shape((2, 2, C, C, 64), F32)),
        in_specs=[anywhere, vmem, vmem],
        out_specs=[anywhere] * 2,
        scratch_shapes=[
            V((ROWS, W), BF),
            V((2, 2, C, C, 64), F32),
            V((2, NQ, NI, KH), F32),
            V((2, NQ, NI, KH), F32),
            V((2, C, KH), F32),
            DMA((NI,)),
            DMA((NI,)),
            DMA((2, 2, NI)),
        ],
        compiler_params=pltpu.CompilerParams(vmem_limit_bytes=56 * 1024 * 1024),
        name="outputs",
    )(surface_gradient, xm, gm)
    return surface_gradient.reshape(1, C, R, W), weight_gradient


def solution(mesh):
    placed = (
        P("batch", None, "rows", None),
        P("batch", None, "rows", None),
        P("rows", None, None, None, "batch"),
        P(),
        P(),
    )
    return jax.shard_map(
        local,
        mesh=mesh,
        in_specs=placed,
        out_specs=(P("batch", None, "rows", None), P("rows", None, None, None, "batch")),
        check_vma=False,
    )
```

time: 144 us -> 119 us (0.83)
  Pallas kernels: 138 us -> 118 us
  local copies, waits for them, and re-layouts: 4.63 us -> 0 us
    pallas_call x1, Pallas kernels: 16.6 us -> 6.29 us  [local(): pl.pallas_call(outputs, out_shape=(shape((ROWS, W), BF), shape((2, 2, C,...]
    pallas_call x1, Pallas kernels: 122 us -> 112 us  [local(): pl.pallas_call(transfers, out_shape=(shape((ROWS, W), BF), shape((2, 2, N...]
    unnamed x12 -> x0, local copies, waits for them, and re-layouts: 4.63 us -> none
where the time goes in v1:
time: 119 us
  Pallas kernels  118 us (99%)
    pallas_call x1, Pallas kernels, local(): pl.pallas_call(transfers, out_shape=(shape((ROWS, W), BF), shape((2, 2, N...  112 us
    pallas_call x1, Pallas kernels, local(): pl.pallas_call(outputs, out_shape=(shape((ROWS, W), BF), shape((2, 2, C,...  6.29 us

profile of v1, /device:TPU:1, one launch (start us, length us, event | category | flops | bytes accessed | tf_op | source)
XLA Modules:
  0.0 118.8 jit_solution(6101882469050698586)
XLA Ops:
  0.6 111.9 %transfers.1 = (bf16[1024,1024]{1,0:T(8,128)(2,1)}, f32[2,2,16,4,128]{4,3,2,1,0:T(4,128)}, f32[2,2,64,128]{3,2,1,0:T(8,128)}) custom-call(bf16[1024,1024]{1,0:T(8,128)(2,1)} %bitcast.4, bf16[1024,1024]{1,0:T(8,128)(2,1)} %bitcast.5, bf16[2,2,64,64,64]{4,3,2,1,0:T(8,128)(2,1)} %w_hbm.1, bf16[1024,512]{1,0:T(8,128)(2,1)} %constant.12.clone.t1_hbm, ...), custom_call_target="tpu_custom_call" | custom-call | tf_op jit(solution)/shard_map/transfers/pallas_call | solution.py:484
  112.5 6.3 %outputs.1 = (bf16[1024,1024]{1,0:T(8,128)(2,1)}, f32[2,2,64,64,64]{4,3,2,1,0:T(8,128)}) custom-call(bf16[1024,1024]{1,0:T(8,128)(2,1)} %get-tuple-element.7.sg_in, f32[2,2,16,4,128]{4,3,2,1,0:T(4,128)} %get-tuple-element.8.xm, f32[2,2,64,128]{3,2,1,0:T(8,128)} %get-tuple-element.9.gm), custom_call_target="tpu_custom_call" | custom-call | tf_op jit(solution)/shard_map/outputs/pallas_call | solution.py:552

commit v2 on v1

--- a/solution.py
+++ b/solution.py
@@ -104,9 +104,9 @@
 
 
 def transfers(
-    x_hbm, cot_hbm, w_hbm, t1_hbm, t1t_hbm, rows_hbm, lw_ref, bias_ref, gather_ref, spread_ref, natural_ref,
+    x_hbm, cot_hbm, w_hbm, t1_hbm, t1t_hbm, rows_hbm, lw_hbm, bias_hbm, gather_hbm, spread_hbm, natural_hbm,
     sg_hbm, xm_hbm, gm_hbm,
-    x, cot, w, t1, t1t, rt, w2r, w2i, kron, pre, slopes,
+    lw_ref, bias_ref, gather_ref, spread_ref, natural_ref, x, cot, w, t1, t1t, rt, w2r, w2i, kron, pre, slopes,
     a_out, a_in, b_out, b_in, c_out, c_in, d_out, d_in, e_out, e_in, f_out, f_in, turned, mixed, nat,
     load, store, sa, ra, sb, rb, sc, rc, sd, rd, se, re, sf, rf,
 ):
@@ -150,13 +150,24 @@
     load_w = pltpu.make_async_copy(w_hbm, w, load.at[6])
     load_t1t = pltpu.make_async_copy(t1t_hbm, t1t, load.at[7])
     load_cot = pltpu.make_async_copy(cot_hbm, cot, load.at[8])
+    smalls = []
+    for n, (src, dst) in enumerate(
+        (
+            (lw_hbm, lw_ref),
+            (bias_hbm, bias_ref),
+            (gather_hbm, gather_ref),
+            (spread_hbm, spread_ref),
+            (natural_hbm, natural_ref),
+        )
+    ):
+        smalls.append(pltpu.make_async_copy(src, dst, load.at[9 + n]))
     load_t1.start()
     for copy in loads:
         copy.start()
     loop(1, NQ, lambda p: greet(b, z * NQ + in_plane(p)))
     loop(0, NQ, lambda p: greet(1 - b, z * NQ + p))
     loop(1, NZ, lambda p: greet(b, along(p) * NQ + q))
-    for copy in (load_rows, load_w, load_t1t, load_cot):
+    for copy in (load_rows, load_w, *smalls, load_t1t, load_cot):
         copy.start()
 
     def split_columns(rnd, i, rows_of):
@@ -170,11 +181,11 @@
     load_t1.wait()
 
     def first(i):
-        part = pl.ds(pl.multiple_of(i * CHUNK, CHUNK), CHUNK)
+        part = pl.ds(pl.multiple_of(jnp.int32(i) * CHUNK, CHUNK), CHUNK)
         pltpu.make_async_copy(x_hbm.at[part], x.at[part], load.at[i]).wait()
         split_columns(0, i, x[part])
 
-    loop(0, NI, first)
+    first(0)
     pl.semaphore_wait(barrier, 2 * NQ - 1 + NZ - 1)
 
     def send_plane(out, into, s, r, rnd, kk, i):
@@ -237,11 +248,12 @@
             d_out[rnd, kk, m] = dot(spread_ref[...], mixed[m].astype(BF)).reshape(NQ, NI, KH)
         send_owners(d_out, d_in, sd, rd, rnd, kk)
 
-    def spread_modes(rnd, kk):
+    def narrow_modes(rnd, kk):
         wait(d_in.at[rnd, kk], rd.at[rnd, kk])
         halves = [dot(natural_ref[...], d_in[rnd, kk, half].reshape(C, KH).astype(BF)) for half in range(2)]
         e_out[rnd, kk] = jnp.concatenate(halves, axis=1).astype(BF).reshape(NI, NQ, 2 * KH)
 
+    def spread_modes(rnd, kk, lo=0, hi=NI):
         def one_channel(i):
             def one(p):
                 to = along(p)
@@ -250,7 +262,7 @@
             loop(1, NZ, one)
             pltpu.make_async_copy(e_out.at[rnd, kk, i], e_in.at[rnd, kk, i, z], re.at[rnd, kk, i]).start()
 
-        loop(0, NI, one_channel)
+        loop(lo, hi, one_channel)
 
     def to_rows(rnd, kk, lo=0, hi=NI):
         def one_channel(i):
@@ -264,13 +276,17 @@
 
         loop(lo, hi, one_channel)
 
-    def from_rows(rnd, i):
+    def row_part(rnd, kk, i):
+        wait(f_in.at[rnd, kk, i], rf.at[rnd, kk, i])
         start = pl.multiple_of(i * CHUNK, CHUNK)
-        total = pre[pl.ds(start, CHUNK)]
-        for kk in range(2):
-            wait(f_in.at[rnd, kk, i], rf.at[rnd, kk, i])
-            total = total + dot(f_in[rnd, kk, i].reshape(CHUNK, 2 * KO), t1t[kk * 256 : (kk + 1) * 256])
-        return total
+        field = dot(f_in[rnd, kk, i].reshape(CHUNK, 2 * KO), t1t[kk * 256 : (kk + 1) * 256])
+        return pre[pl.ds(start, CHUNK)] + field
+
+    def add_even(rnd):
+        def one_channel(i):
+            pre[pl.ds(pl.multiple_of(i * CHUNK, CHUNK), CHUNK)] = row_part(rnd, 0, i)
+
+        loop(0, NI, one_channel)
 
     def pointwise(rnd, lo, hi):
         field, over = ((x, 1), (slopes, 0))[rnd]
@@ -334,10 +350,17 @@
 
         loop(0, C // 8, terms)
 
-    for i in range(NI):
+    send_plane(a_out, a_in, sa, ra, 0, 0, 0)
+
+    def first_and_send(i):
+        first(i)
         send_plane(a_out, a_in, sa, ra, 0, 0, i)
+
+    loop(1, NI, first_and_send)
     load_w.wait()
     loop(0, 24, widen)
+    for copy in smalls:
+        copy.wait()
     for i in range(NI):
         sent_plane(a_out, sa, 0, 0, i)
         send_plane(a_out, a_in, sa, ra, 0, 1, i)
@@ -349,15 +372,17 @@
     to_modes(0, 1)
     to_owners(0, 0)
     loop(40, C, widen)
-    to_owners(0, 1)
     mix(0)
     from_owners(0, 0)
-    pointwise(0, 2, 3)
+    to_owners(0, 1)
+    pointwise(0, 2, 4)
+    narrow_modes(0, 0)
+    spread_modes(0, 0, 0, 2)
     mix(1)
     from_owners(0, 1)
-    pointwise(0, 3, 4)
-    spread_modes(0, 0)
+    spread_modes(0, 0, 2, 4)
     to_rows(0, 0, 0, 2)
+    narrow_modes(0, 1)
     spread_modes(0, 1)
     to_rows(0, 0, 2, 4)
     to_rows(0, 1)
@@ -365,12 +390,13 @@
     copy_xm.start()
 
     load_t1t.wait()
+    add_even(0)
     load_cot.wait()
 
     def second(i):
         start = pl.multiple_of(i * CHUNK, CHUNK)
         part = pl.ds(start, CHUNK)
-        pre[part] = from_rows(0, i)
+        pre[part] = row_part(0, 1, i)
 
         def slab(s):
             at = pl.ds(pl.multiple_of(start + s * 16, 16), 16)
@@ -386,25 +412,27 @@
     to_modes(1, 0)
     to_modes(1, 1)
     to_owners(1, 0)
-    pointwise(1, 0, 2)
-    to_owners(1, 1)
+    pointwise(1, 0, 4)
     mix_back(0)
     from_owners(1, 0)
-    pointwise(1, 2, 3)
+    to_owners(1, 1)
+    narrow_modes(1, 0)
+    spread_modes(1, 0, 0, 2)
     mix_back(1)
     from_owners(1, 1)
-    pointwise(1, 3, 4)
-    spread_modes(1, 0)
+    spread_modes(1, 0, 2, 4)
     to_rows(1, 0, 0, 2)
+    narrow_modes(1, 1)
     spread_modes(1, 1)
     to_rows(1, 0, 2, 4)
     to_rows(1, 1)
+    add_even(1)
     copy_gm = pltpu.make_async_copy(nat, gm_hbm, store.at[NI + 1])
     copy_gm.start()
 
     def last(i):
         part = pl.ds(pl.multiple_of(i * CHUNK, CHUNK), CHUNK)
-        x[part] = from_rows(1, i).astype(BF)
+        x[part] = row_part(1, 1, i).astype(BF)
         pltpu.make_async_copy(x.at[part], sg_hbm.at[part], store.at[i]).start()
 
     loop(0, NI, last)
@@ -430,7 +458,10 @@
                 wait(out.at[rnd, kk, 0], s.at[rnd, kk, 1])
 
 
-def outputs(sg_in, xm, gm, sg_hbm, wg_hbm, sg, wg, xr, xi, turned, load, store_s, store_w):
+def outputs(sg_in, xm_hbm, gm_hbm, sg_hbm, wg_hbm, xm, gm, sg, wg, xr, xi, turned, load, store_s, store_w):
+    modes = [pltpu.make_async_copy(xm_hbm, xm, load.at[NI]), pltpu.make_async_copy(gm_hbm, gm, load.at[NI + 1])]
+    for copy in modes:
+        copy.start()
     loads, passes = [], []
     for n in range(NI):
         part = pl.ds(n * CHUNK, CHUNK)
@@ -439,6 +470,8 @@
         loads[n].start()
     low = lax.broadcasted_iota(jnp.int32, (C, KH), 1) < 64
     stores = []
+    for copy in modes:
+        copy.wait()
     for kk in range(2):
         for m in range(2):
             rows_of = xm[kk, m].reshape(C, KH)
@@ -477,7 +510,6 @@
     row_table = jnp.asarray(rows, BF)
     gather, spread, natural = (jnp.asarray(p, BF) for p in permutations())
     anywhere = pl.BlockSpec(memory_space=pl.ANY)
-    vmem = pl.BlockSpec(memory_space=pltpu.VMEM)
     DMA = pltpu.SemaphoreType.DMA
     V = pltpu.VMEM
     shape = jax.ShapeDtypeStruct
@@ -488,9 +520,14 @@
             shape((2, 2, NQ, NI, KH), F32),
             shape((2, 2, C, KH), F32),
         ),
-        in_specs=[anywhere] * 6 + [vmem] * 5,
+        in_specs=[anywhere] * 11,
         out_specs=[anywhere] * 3,
         scratch_shapes=[
+            V((C, C), BF),
+            V((1, C), F32),
+            V((64, 512), BF),
+            V((64, 64), BF),
+            V((64, 64), BF),
             V((ROWS, W), BF),
             V((ROWS, W), BF),
             V((2, 2, C, C, 64), BF),
@@ -517,7 +554,7 @@
             V((2, NQ, NI, KH), F32),
             V((2, C, KH), F32),
             V((2, 2, C, KH), F32),
-            DMA((9,)),
+            DMA((14,)),
             DMA((NI + 2,)),
             DMA((2, 2, NI)),
             DMA((2, 2, NI)),
@@ -552,15 +589,17 @@
     surface_gradient, weight_gradient = pl.pallas_call(
         outputs,
         out_shape=(shape((ROWS, W), BF), shape((2, 2, C, C, 64), F32)),
-        in_specs=[anywhere, vmem, vmem],
+        in_specs=[anywhere] * 3,
         out_specs=[anywhere] * 2,
         scratch_shapes=[
+            V((2, 2, NQ, NI, KH), F32),
+            V((2, 2, C, KH), F32),
             V((ROWS, W), BF),
             V((2, 2, C, C, 64), F32),
             V((2, NQ, NI, KH), F32),
             V((2, NQ, NI, KH), F32),
             V((2, C, KH), F32),
-            DMA((NI,)),
+            DMA((NI + 2,)),
             DMA((NI,)),
             DMA((2, 2, NI)),
         ],

time: 119 us -> 116 us (0.975)
  Pallas kernels: 118 us -> 115 us
    pallas_call x1, Pallas kernels: 112 us -> 109 us  [local(): pl.pallas_call(transfers, out_shape=(shape((ROWS, W), BF), shape((2, 2, N...]
where the time goes in v2:
time: 116 us
  Pallas kernels  115 us (99%)
    pallas_call x1, Pallas kernels, local(): pl.pallas_call(transfers, out_shape=(shape((ROWS, W), BF), shape((2, 2, N...  109 us
    pallas_call x1, Pallas kernels, local(): pl.pallas_call(outputs, out_shape=(shape((ROWS, W), BF), shape((2, 2, C,...  5.8 us

profile of v2, /device:TPU:1, one launch (start us, length us, event | category | flops | bytes accessed | tf_op | source)
XLA Modules:
  0.0 115.6 jit_solution(1275297347943295375)
XLA Ops:
  0.6 109.1 %transfers.1 = (bf16[1024,1024]{1,0:T(8,128)(2,1)}, f32[2,2,16,4,128]{4,3,2,1,0:T(4,128)}, f32[2,2,64,128]{3,2,1,0:T(8,128)}) custom-call(bf16[1024,1024]{1,0:T(8,128)(2,1)} %bitcast.4, bf16[1024,1024]{1,0:T(8,128)(2,1)} %bitcast.5, bf16[2,2,64,64,64]{4,3,2,1,0:T(8,128)(2,1)} %w_hbm.1, bf16[1024,512]{1,0:T(8,128)(2,1)} %constant.12.clone.t1_hbm, ...), custom_call_target="tpu_custom_call" | custom-call | tf_op jit(solution)/shard_map/transfers/pallas_call | solution.py:516
  109.8 5.8 %outputs.1 = (bf16[1024,1024]{1,0:T(8,128)(2,1)}, f32[2,2,64,64,64]{4,3,2,1,0:T(8,128)}) custom-call(bf16[1024,1024]{1,0:T(8,128)(2,1)} %get-tuple-element.7.sg_in, f32[2,2,16,4,128]{4,3,2,1,0:T(4,128)} %get-tuple-element.8.xm_hbm, f32[2,2,64,128]{3,2,1,0:T(8,128)} %get-tuple-element.9.gm_hbm), custom_call_target="tpu_custom_call" | custom-call | tf_op jit(solution)/shard_map/outputs/pallas_call | solution.py:589

commit v3 on v2

v3 whole, which is shorter than its diff:
```python
import math

import jax
import jax.numpy as jnp
import numpy as np
from jax import lax
from jax.experimental import pallas as pl
from jax.experimental.pallas import tpu as pltpu
from jax.sharding import PartitionSpec as P

MESH = pl.DeviceIdType.MESH
BF = jnp.bfloat16
F32 = jnp.float32

C = 64
R = 16
W = 1024
KW = 256
KH = 128
NZ = 8
NQ = 16
NH = 8
NU = 4
NI = 4
ROWS = C * R
CHUNK = NQ * R


def tables():
    w = np.arange(W)[:, None]
    columns = []
    for u in range(NU):
        owner = (NQ * np.arange(NZ)[:, None] + NH * (u % 2) + np.arange(NH)[None, :]).reshape(1, -1)
        k = 2 * owner + u // 2
        angle = 2 * np.pi * ((w * k) % W) / W
        columns += [np.cos(angle), -np.sin(angle)]
    columns = np.concatenate(columns, axis=1)
    height = NZ * NQ * R
    jj = np.arange(KH // 2)
    rows = np.zeros((NZ, CHUNK, 4 * KH))
    for z in range(NZ):
        h = (z * CHUNK + np.arange(CHUNK))[:, None]
        for half in range(2):
            f = (jj - half * (KH // 2))[None, :]
            angle = 2 * np.pi * ((f * h) % height) / height
            cos, sin = np.cos(angle), np.sin(angle)
            at = half * KH
            rows[z, :, at : at + 64] = cos
            rows[z, :, at + 64 : at + 128] = -sin
            rows[z, :, 256 + at : 256 + at + 64] = sin
            rows[z, :, 256 + at + 64 : 256 + at + 128] = cos
    return columns, rows


def permutations():
    gather = np.zeros((NH, NI, 2, NZ, 2, NH))
    spread = np.zeros((NQ, NI, C))
    modes = np.zeros((NI, NH, NH, NI))
    planes = np.zeros((2, NZ, NH, NZ, 2, NH))
    for i in range(NI):
        for q in range(NQ):
            spread[q, i, 16 * i + q] = 1
        for q in range(NH):
            gather[q, i, i // 2, :, i % 2, q] = 1
            modes[i, q, q, i] = 1
            for z in range(NZ):
                planes[i % 2, z, q, z, i % 2, q] = 1
    spread = spread.reshape(64, 64)
    return gather.reshape(32, 256), spread, spread.T.copy(), modes.reshape(32, 32), planes.reshape(128, 128)


def dot(a, b, ca=1, cb=0):
    return lax.dot_general(a, b, (((ca,), (cb,)), ((), ())), preferred_element_type=F32)


def gelu_slope(v):
    cumulative = 0.5 * (1.0 + lax.erf(v * (1.0 / math.sqrt(2.0))))
    density = jnp.exp(-0.5 * v * v) * (1.0 / math.sqrt(2.0 * math.pi))
    return cumulative + v * density


def expand_matrix(start):
    row = lax.broadcasted_iota(jnp.int32, (CHUNK, C), 0) + start
    col = lax.broadcasted_iota(jnp.int32, (CHUNK, C), 1)
    return (row // R == col).astype(F32).astype(BF)


def same_row_mask():
    row = lax.broadcasted_iota(jnp.int32, (CHUNK, CHUNK), 0) % R
    col = lax.broadcasted_iota(jnp.int32, (CHUNK, CHUNK), 1) % R
    return row == col


def mix_rows(weight_rows):
    mask = same_row_mask()
    for i in range(NI):
        spread = dot(weight_rows, expand_matrix(i * CHUNK), 1, 1)
        yield i, jnp.where(mask, spread, 0.0).astype(BF)


def column_scale(u):
    if u:
        return jnp.full((1, 128), 2.0**-20, F32)
    lane = lax.broadcasted_iota(jnp.int32, (1, 128), 1)
    return jnp.where(lane % 64 == 0, 2.0**-21, 2.0**-20).astype(F32)


def half_sign():
    lane = lax.broadcasted_iota(jnp.int32, (1, 128), 1)
    return jnp.where(lane < 64, -1.0, 1.0).astype(F32)


def transfers(
    x_hbm, cot_hbm, w_hbm, t1_hbm, t1t_hbm, rows_hbm, lw_hbm, bias_hbm, gather_hbm, spread_hbm, natural_hbm, modes_hbm,
    planes_hbm,
    sg_hbm, xm_hbm, gm_hbm,
    lw_ref, bias_ref, gather_ref, spread_ref, natural_ref, modes_ref, planes_ref, x, cot, w, t1, t1t, rt, w2r, w2i, kron, pre, slopes,
    a_out, a_in, b_out, b_in, c_out, c_in, d_out, d_in, e_out, e_in, f_out, f_in, turned, mixed, nat,
    load, store, sa, ra, sb, rb, sc, rc, sd, rd, se, re, sf, rf,
):
    b = lax.axis_index("batch")
    d = lax.axis_index("rows")
    z = d // NQ
    q = d % NQ
    qh = q // NH
    q8 = q % NH

    def in_plane(p):
        return lax.rem(q + p, NQ)

    def along(p):
        return lax.rem(z + p, NZ)

    def wait(ref, sem):
        pltpu.make_async_copy(ref, ref, sem).wait()

    def send(src, dst, s, r, batch, row):
        pltpu.make_async_remote_copy(
            src_ref=src, dst_ref=dst, send_sem=s, recv_sem=r, device_id=(batch, row), device_id_type=MESH
        ).start()

    def loop(lo, hi, body):
        def step(p, carry):
            body(p)
            return carry

        lax.fori_loop(lo, hi, step, 0)

    barrier = pltpu.get_barrier_semaphore()

    def greet(batch, row):
        pl.semaphore_signal(barrier, inc=1, device_id=(batch, row), device_id_type=MESH)

    loads = []
    for i in range(NI):
        part = pl.ds(i * CHUNK, CHUNK)
        loads.append(pltpu.make_async_copy(x_hbm.at[part], x.at[part], load.at[i]))
    load_t1 = pltpu.make_async_copy(t1_hbm, t1, load.at[4])
    load_rows = pltpu.make_async_copy(rows_hbm.at[z], rt, load.at[5])
    load_w = pltpu.make_async_copy(w_hbm, w, load.at[6])
    load_t1t = pltpu.make_async_copy(t1t_hbm, t1t, load.at[7])
    load_cot = pltpu.make_async_copy(cot_hbm, cot, load.at[8])
    smalls = []
    for n, (src, dst) in enumerate(
        (
            (lw_hbm, lw_ref),
            (bias_hbm, bias_ref),
            (gather_hbm, gather_ref),
            (spread_hbm, spread_ref),
            (natural_hbm, natural_ref),
            (modes_hbm, modes_ref),
            (planes_hbm, planes_ref),
        )
    ):
        smalls.append(pltpu.make_async_copy(src, dst, load.at[9 + n]))
    load_t1.start()
    for copy in loads:
        copy.start()
    loop(1, NQ, lambda p: greet(b, z * NQ + in_plane(p)))
    loop(0, NQ, lambda p: greet(1 - b, z * NQ + p))
    loop(1, NZ, lambda p: greet(b, along(p) * NQ + q))
    for copy in (load_rows, load_w, *smalls, load_t1t, load_cot):
        copy.start()

    def split_columns(rnd, ip, i2, rows_of, lo=0, hi=NU):
        field = dot(rows_of, t1[:, lo * 128 : hi * 128])
        for u in range(lo, hi):
            part = field[:, (u - lo) * 128 : (u - lo + 1) * 128]
            if rnd:
                part = part * column_scale(u)
            a_out[rnd, u, ip, :, i2] = part.astype(BF).reshape(NQ, R, 128)

    load_t1.wait()

    def first(ip):
        for i2 in range(2):
            part = pl.ds((2 * ip + i2) * CHUNK, CHUNK)
            loads[2 * ip + i2].wait()
            split_columns(0, ip, i2, x[part])

    first(0)
    pl.semaphore_wait(barrier, 2 * NQ - 1 + NZ - 1)

    def send_plane(out, into, s, r, rnd, u, ip):
        def one(p):
            to = in_plane(p)
            send(
                out.at[rnd, u, ip, to], into.at[rnd, u, ip, q], s.at[rnd, u, ip], r.at[rnd, u, ip], b, z * NQ + to
            )

        loop(1, NQ, one)
        pltpu.make_async_copy(out.at[rnd, u, ip, q], into.at[rnd, u, ip, q], r.at[rnd, u, ip]).start()

    def send_channel(rnd, u, ip, i2):
        def one(p):
            to = in_plane(p)
            send(
                a_out.at[rnd, u, ip, to, i2], a_in.at[rnd, u, ip, q, i2], sa.at[rnd, u, ip], ra.at[rnd, u, ip],
                b, z * NQ + to,
            )

        loop(1, NQ, one)
        pltpu.make_async_copy(a_out.at[rnd, u, ip, q, i2], a_in.at[rnd, u, ip, q, i2], ra.at[rnd, u, ip]).start()

    def sent_plane(out, s, rnd, u, ip):
        wait(out.at[rnd, u, ip, pl.ds(0, NQ - 1)], s.at[rnd, u, ip])

    def to_modes(rnd, u, lo=0, hi=2):
        def two_channels(ip):
            wait(a_in.at[rnd, u, ip], ra.at[rnd, u, ip])
            terms = []
            for i2 in range(2):
                both = dot(a_in[rnd, u, ip, :, i2].reshape(CHUNK, 128), rt[...], 0, 0)
                term = both[:64, : 2 * KH] + both[64:, 2 * KH :]
                terms.append(term.reshape(NZ, NH, 2 * KH))
            b_out[rnd, u, ip] = jnp.concatenate(terms, axis=1).astype(BF)

            def one(p):
                to = along(p)
                send(
                    b_out.at[rnd, u, ip, to], b_in.at[rnd, u, ip, z], sb.at[rnd, u, ip], rb.at[rnd, u], b, to * NQ + q
                )

            loop(1, NZ, one)
            pltpu.make_async_copy(b_out.at[rnd, u, ip, z], b_in.at[rnd, u, ip, z], rb.at[rnd, u]).start()

        loop(lo, hi, two_channels)

    def to_owners(rnd, u):
        kk, h = u // 2, u % 2
        wait(b_in.at[rnd, u], rb.at[rnd, u])
        total = dot(gather_ref[...], b_in[rnd, u].reshape(256, 2 * KH))
        for half in range(2):
            c_out[rnd, u, half] = total[:, half * KH : (half + 1) * KH].reshape(NH, NI, KH)

        def other(p):
            to = lax.rem(q8 + p, NH)
            row = z * NQ + h * NH + to
            send(c_out.at[rnd, u, 1 - b, to], c_in.at[rnd, kk, b, q], sc.at[rnd, u, 1], rc.at[rnd, kk], 1 - b, row)

        def same(p):
            to = lax.rem(q8 + p, NH)
            row = z * NQ + h * NH + to
            send(c_out.at[rnd, u, b, to], c_in.at[rnd, kk, b, q], sc.at[rnd, u, 0], rc.at[rnd, kk], b, row)

        loop(0, NH, other)
        loop(1, NH, same)

        @pl.when(qh != h)
        def _():
            same(0)

        @pl.when(qh == h)
        def _():
            pltpu.make_async_copy(c_out.at[rnd, u, b, q8], c_in.at[rnd, kk, b, q], rc.at[rnd, kk]).start()

    def at_owners(rnd, u):
        @pl.when(qh == u % 2)
        def _():
            (mix, mix_back)[rnd](u // 2)
            from_owners(rnd, u)

    def from_owners(rnd, u):
        kk = u // 2
        for m in range(2):
            d_out[rnd, kk, m] = dot(spread_ref[...], mixed[m].astype(BF)).reshape(NQ, NI, KH)

        def other(p):
            to = in_plane(p)
            row = z * NQ + to
            send(d_out.at[rnd, kk, 1 - b, to], d_in.at[rnd, u, b, q8], sd.at[rnd, kk, 1], rd.at[rnd, u], 1 - b, row)

        def same(p):
            to = in_plane(p)
            row = z * NQ + to
            send(d_out.at[rnd, kk, b, to], d_in.at[rnd, u, b, q8], sd.at[rnd, kk, 0], rd.at[rnd, u], b, row)

        loop(0, NQ, other)
        loop(1, NQ, same)
        pltpu.make_async_copy(d_out.at[rnd, kk, b, q], d_in.at[rnd, u, b, q8], rd.at[rnd, u]).start()

    def spread_modes(rnd, u):
        wait(d_in.at[rnd, u], rd.at[rnd, u])
        halves = [dot(modes_ref[...], d_in[rnd, u, half].reshape(32, KH).astype(BF)) for half in range(2)]
        e_out[rnd, u] = jnp.concatenate(halves, axis=1).astype(BF).reshape(2, 2 * NH, 2 * KH)
        for op in range(2):

            def one(p):
                to = along(p)
                send(e_out.at[rnd, u, op], e_in.at[rnd, u, op, z], se.at[rnd, u, op], re.at[rnd, u, op], b, to * NQ + q)

            loop(1, NZ, one)
            pltpu.make_async_copy(e_out.at[rnd, u, op], e_in.at[rnd, u, op, z], re.at[rnd, u, op]).start()

    def to_rows(rnd, u):
        def two_channels(op):
            wait(e_in.at[rnd, u, op], re.at[rnd, u, op])
            spectra = dot(planes_ref[...], e_in[rnd, u, op].reshape(128, 2 * KH)).astype(BF)
            real = dot(rt[:, : 2 * KH], spectra, 1, 1)
            imag = dot(rt[:, 2 * KH :], spectra, 1, 1)
            for o2 in range(2):
                at = slice(64 * o2, 64 * o2 + 64)
                both = jnp.concatenate([real[:, at], imag[:, at]], axis=1)
                if rnd == 0:
                    both = both * column_scale(u)
                f_out[rnd, u, op, :, o2] = both.astype(BF).reshape(NQ, R, 128)
            send_plane(f_out, f_in, sf, rf, rnd, u, op)

        loop(0, 2, two_channels)

    def row_parts(rnd, kk, op):
        us = (2 * kk, 2 * kk + 1)
        for u in us:
            wait(f_in.at[rnd, u, op], rf.at[rnd, u, op])
        for o2 in range(2):
            start = pl.multiple_of((2 * op + o2) * CHUNK, CHUNK)
            part = pl.ds(start, CHUNK)
            rows_of = jnp.concatenate([f_in[rnd, u, op, :, o2].reshape(CHUNK, 128) for u in us], axis=1)
            yield start, part, pre[part] + dot(rows_of, t1t[kk * 256 : (kk + 1) * 256])

    def add_even(rnd):
        def two_channels(op):
            for _, part, total in row_parts(rnd, 0, op):
                pre[part] = total

        loop(0, 2, two_channels)

    def pointwise(rnd, lo, hi):
        field, over = ((x, 1), (slopes, 0))[rnd]

        def rows_of_one(n):
            start = pl.multiple_of(n * CHUNK, CHUNK)
            mine = expand_matrix(start)
            for i, block in mix_rows(dot(mine, lw_ref[...], 1, over).astype(BF)):
                kron[:, i * CHUNK : (i + 1) * CHUNK] = block
            part = pl.ds(start, CHUNK)
            pre[part] = dot(kron[...], field[...])
            if rnd == 0:
                pre[part] += jnp.sum(mine.astype(F32) * bias_ref[...], axis=1, keepdims=True)

        loop(lo, hi, rows_of_one)

    def widen(c):
        for kk in range(2):
            for part, wide in enumerate((w2r, w2i)):
                block = w[kk, part, c].astype(F32)
                wide[kk, c] = jnp.concatenate([block, block], axis=1)

    def mix(kk):
        wait(c_in.at[0, kk], rc.at[0, kk])
        for m in range(2):
            rows_of = c_in[0, kk, m].reshape(C, KH)
            turned[m] = (pltpu.roll(rows_of, 64, 1) * half_sign()).reshape(NQ, NI, KH)

        def terms(qq, sums):
            sums = list(sums)
            for i in range(NI):
                real = w2r[kk, 16 * i + qq]
                imag = w2i[kk, 16 * i + qq]
                for m in range(2):
                    sums[m] = sums[m] + c_in[0, kk, m, qq, i : i + 1] * real + turned[m, qq, i : i + 1] * imag
            return tuple(sums)

        sums = lax.fori_loop(0, NQ, terms, (jnp.zeros((C, KH), F32),) * 2)
        for m in range(2):
            mixed[m] = sums[m]

    def mix_back(kk):
        wait(c_in.at[1, kk], rc.at[1, kk])
        grads = []
        grads_turned = []
        for m in range(2):
            grads.append(dot(natural_ref[...], c_in[1, kk, m].reshape(C, KH).astype(BF)))
            grads_turned.append(pltpu.roll(grads[m], 64, 1) * -half_sign())
            nat[kk, m] = grads[m]

        def terms(c8):
            rows_of = ([], [])
            for n in range(8):
                c = c8 * 8 + n
                real = w2r[kk, c]
                imag = w2i[kk, c]
                for m in range(2):
                    rows_of[m].append(jnp.sum(grads[m] * real + grads_turned[m] * imag, axis=0, keepdims=True))
            for m in range(2):
                mixed[m, pl.ds(pl.multiple_of(c8 * 8, 8), 8)] = jnp.concatenate(rows_of[m], axis=0)

        loop(0, C // 8, terms)

    def transforms(rnd, last_modes, spares):
        to_owners(rnd, 0)
        last_modes(2)
        if rnd == 0:
            loop(48, C, widen)
        to_owners(rnd, 1)
        last_modes(3)
        spares(0)
        at_owners(rnd, 0)
        to_owners(rnd, 2)
        spares(1)
        at_owners(rnd, 1)
        to_owners(rnd, 3)
        spread_modes(rnd, 0)
        at_owners(rnd, 2)
        spread_modes(rnd, 1)
        at_owners(rnd, 3)
        to_rows(rnd, 0)
        spread_modes(rnd, 2)
        to_rows(rnd, 1)
        spread_modes(rnd, 3)
        to_rows(rnd, 2)
        to_rows(rnd, 3)
        spares(2)
        spares(3)
        add_even(rnd)

    def next_piece(rnd, n):
        sent_plane(a_out, sa, rnd, (n - 2) // 2, n % 2)
        send_plane(a_out, a_in, sa, ra, rnd, n // 2, n % 2)

    send_plane(a_out, a_in, sa, ra, 0, 0, 0)
    first(1)
    send_plane(a_out, a_in, sa, ra, 0, 0, 1)
    load_w.wait()
    for copy in smalls:
        copy.wait()
    loop(0, 16, widen)
    next_piece(0, 2)
    loop(16, 32, widen)
    next_piece(0, 3)
    load_rows.wait()
    to_modes(0, 0, 0, 1)
    next_piece(0, 4)
    to_modes(0, 0, 1, 2)
    next_piece(0, 5)
    loop(32, 48, widen)
    to_modes(0, 1, 0, 1)
    next_piece(0, 6)
    to_modes(0, 1, 1, 2)
    next_piece(0, 7)
    load_t1t.wait()
    transforms(0, lambda u: to_modes(0, u), lambda n: pointwise(0, n, n + 1))
    copy_xm = pltpu.make_async_copy(c_in.at[0], xm_hbm, store.at[NI])
    copy_xm.start()

    load_cot.wait()

    def second(op):
        for o2, (start, part, total) in enumerate(row_parts(0, 1, op)):
            pre[part] = total

            def slab(s):
                at = pl.ds(pl.multiple_of(start + s * 16, 16), 16)
                slopes[at] = (cot[at].astype(F32) * gelu_slope(pre[at])).astype(BF)

            loop(0, CHUNK // 16, slab)
            split_columns(1, op, o2, slopes[part], 0, 1)
            send_channel(1, 0, op, o2)

    def other_quarters(op):
        for o2 in range(2):
            start = pl.multiple_of((2 * op + o2) * CHUNK, CHUNK)
            split_columns(1, op, o2, slopes[pl.ds(start, CHUNK)], 1, NU)
        send_plane(a_out, a_in, sa, ra, 1, 1, op)

    loop(0, 2, second)
    loop(0, 2, other_quarters)
    to_modes(1, 0, 0, 1)
    next_piece(1, 4)
    to_modes(1, 0, 1, 2)
    next_piece(1, 5)
    to_modes(1, 1, 0, 1)
    next_piece(1, 6)
    to_modes(1, 1, 1, 2)
    next_piece(1, 7)
    transforms(1, lambda u: to_modes(1, u), lambda n: pointwise(1, n, n + 1))
    copy_gm = pltpu.make_async_copy(nat, gm_hbm, store.at[NI + 1])
    copy_gm.start()

    def last(op):
        for o2, (_, part, total) in enumerate(row_parts(1, 1, op)):
            x[part] = total.astype(BF)
            pltpu.make_async_copy(x.at[part], sg_hbm.at[part], store.at[2 * op + o2]).start()

    loop(0, 2, last)

    for i in range(NI):
        part = pl.ds(i * CHUNK, CHUNK)
        pltpu.make_async_copy(x.at[part], sg_hbm.at[part], store.at[i]).wait()
    copy_xm.wait()
    copy_gm.wait()
    for rnd in range(2):
        for u in range(NU):
            for ip in range(2):
                sent_plane(f_out, sf, rnd, u, ip)
                wait(b_out.at[rnd, u, ip, pl.ds(0, NZ - 1)], sb.at[rnd, u, ip])
                wait(e_in.at[rnd, u, ip, pl.ds(0, NZ - 1)], se.at[rnd, u, ip])
                if u == NU - 1 or (rnd == 1 and u == 0):
                    sent_plane(a_out, sa, rnd, u, ip)
            wait(c_out.at[rnd, u, 0], sc.at[rnd, u, 1])

            @pl.when(qh != u % 2)
            def _():
                wait(c_out.at[rnd, u, 0], sc.at[rnd, u, 0])

            @pl.when(qh == u % 2)
            def _():
                wait(c_out.at[rnd, u, 0, pl.ds(0, NH - 1)], sc.at[rnd, u, 0])

        for kk in range(2):
            wait(d_out.at[rnd, kk, 0, pl.ds(0, NQ - 1)], sd.at[rnd, kk, 0])
            wait(d_out.at[rnd, kk, 0], sd.at[rnd, kk, 1])


def outputs(sg_in, xm_hbm, gm_hbm, sg_hbm, wg_hbm, xm, gm, sg, wg, xr, xi, turned, load, store_s, store_w):
    modes = [pltpu.make_async_copy(xm_hbm, xm, load.at[NI]), pltpu.make_async_copy(gm_hbm, gm, load.at[NI + 1])]
    for copy in modes:
        copy.start()
    loads, passes = [], []
    for n in range(NI):
        part = pl.ds(n * CHUNK, CHUNK)
        loads.append(pltpu.make_async_copy(sg_in.at[part], sg.at[part], load.at[n]))
        passes.append(pltpu.make_async_copy(sg.at[part], sg_hbm.at[part], store_s.at[n]))
        loads[n].start()
    low = lax.broadcasted_iota(jnp.int32, (C, KH), 1) < 64
    stores = []
    for copy in modes:
        copy.wait()
    for kk in range(2):
        for m in range(2):
            rows_of = xm[kk, m].reshape(C, KH)
            swapped = pltpu.roll(rows_of, 64, 1)
            xr[m] = jnp.where(low, rows_of, swapped).reshape(NQ, NI, KH)
            xi[m] = jnp.where(low, swapped, rows_of).reshape(NQ, NI, KH)
            turned[m] = pltpu.roll(gm[kk, m], 64, 1) * -half_sign()
        for i in range(NI):

            def terms(q4, carry):
                for n in range(4):
                    qq = q4 * 4 + n
                    total = jnp.zeros((C, KH), F32)
                    for m in range(2):
                        total = total + xr[m, qq, i : i + 1] * gm[kk, m] + xi[m, qq, i : i + 1] * turned[m]
                    wg[kk, 0, 16 * i + qq] = total[:, :64]
                    wg[kk, 1, 16 * i + qq] = total[:, 64:]
                return carry

            lax.fori_loop(0, NQ // 4, terms, 0)
            for part in range(2):
                block = (kk, part, pl.ds(16 * i, 16))
                stores.append(pltpu.make_async_copy(wg.at[block], wg_hbm.at[block], store_w.at[kk, part, i]))
                stores[-1].start()
            if kk == 0:
                loads[i].wait()
                passes[i].start()
    for store in stores + passes:
        store.wait()


def local(surface, cotangent, spectral_weight, local_weight, bias_vector):
    columns, rows = tables()
    t1 = jnp.asarray(columns, BF)
    t1t = jnp.asarray(columns.T, BF)
    row_table = jnp.asarray(rows, BF)
    gather, spread, natural, modes, planes = (jnp.asarray(p, BF) for p in permutations())
    anywhere = pl.BlockSpec(memory_space=pl.ANY)
    DMA = pltpu.SemaphoreType.DMA
    V = pltpu.VMEM
    shape = jax.ShapeDtypeStruct
    surface_gradient, xm, gm = pl.pallas_call(
        transfers,
        out_shape=(
            shape((ROWS, W), BF),
            shape((2, 2, NQ, NI, KH), F32),
            shape((2, 2, C, KH), F32),
        ),
        in_specs=[anywhere] * 13,
        out_specs=[anywhere] * 3,
        scratch_shapes=[
            V((C, C), BF),
            V((1, C), F32),
            V((32, 256), BF),
            V((64, 64), BF),
            V((64, 64), BF),
            V((32, 32), BF),
            V((128, 128), BF),
            V((ROWS, W), BF),
            V((ROWS, W), BF),
            V((2, 2, C, C, 64), BF),
            V((W, 2 * KW), BF),
            V((2 * KW, W), BF),
            V((CHUNK, 4 * KH), BF),
            V((2, C, C, KH), F32),
            V((2, C, C, KH), F32),
            V((CHUNK, ROWS), BF),
            V((ROWS, W), F32),
            V((ROWS, W), BF),
            V((2, NU, 2, NQ, 2, R, 128), BF),
            V((2, NU, 2, NQ, 2, R, 128), BF),
            V((2, NU, 2, NZ, 2 * NH, 2 * KH), BF),
            V((2, NU, 2, NZ, 2 * NH, 2 * KH), BF),
            V((2, NU, 2, NH, NI, KH), F32),
            V((2, 2, 2, NQ, NI, KH), F32),
            V((2, 2, 2, NQ, NI, KH), F32),
            V((2, NU, 2, NH, NI, KH), F32),
            V((2, NU, 2, 2 * NH, 2 * KH), BF),
            V((2, NU, 2, NZ, 2 * NH, 2 * KH), BF),
            V((2, NU, 2, NQ, 2, R, 128), BF),
            V((2, NU, 2, NQ, 2, R, 128), BF),
            V((2, NQ, NI, KH), F32),
            V((2, C, KH), F32),
            V((2, 2, C, KH), F32),
            DMA((16,)),
            DMA((NI + 2,)),
            DMA((2, NU, 2)),
            DMA((2, NU, 2)),
            DMA((2, NU, 2)),
            DMA((2, NU)),
            DMA((2, NU, 2)),
            DMA((2, 2)),
            DMA((2, 2, 2)),
            DMA((2, NU)),
            DMA((2, NU, 2)),
            DMA((2, NU, 2)),
            DMA((2, NU, 2)),
            DMA((2, NU, 2)),
        ],
        compiler_params=pltpu.CompilerParams(
            collective_id=0, has_side_effects=True, vmem_limit_bytes=56 * 1024 * 1024
        ),
        name="transfers",
    )(
        surface.reshape(ROWS, W),
        cotangent.reshape(ROWS, W),
        spectral_weight,
        t1,
        t1t,
        row_table,
        local_weight,
        bias_vector.reshape(1, C),
        gather,
        spread,
        natural,
        modes,
        planes,
    )
    surface_gradient, weight_gradient = pl.pallas_call(
        outputs,
        out_shape=(shape((ROWS, W), BF), shape((2, 2, C, C, 64), F32)),
        in_specs=[anywhere] * 3,
        out_specs=[anywhere] * 2,
        scratch_shapes=[
            V((2, 2, NQ, NI, KH), F32),
            V((2, 2, C, KH), F32),
            V((ROWS, W), BF),
            V((2, 2, C, C, 64), F32),
            V((2, NQ, NI, KH), F32),
            V((2, NQ, NI, KH), F32),
            V((2, C, KH), F32),
            DMA((NI + 2,)),
            DMA((NI,)),
            DMA((2, 2, NI)),
        ],
        compiler_params=pltpu.CompilerParams(vmem_limit_bytes=56 * 1024 * 1024),
        name="outputs",
    )(surface_gradient, xm, gm)
    return surface_gradient.reshape(1, C, R, W), weight_gradient


def solution(mesh):
    placed = (
        P("batch", None, "rows", None),
        P("batch", None, "rows", None),
        P("rows", None, None, None, "batch"),
        P(),
        P(),
    )
    return jax.shard_map(
        local,
        mesh=mesh,
        in_specs=placed,
        out_specs=(P("batch", None, "rows", None), P("rows", None, None, None, "batch")),
        check_vma=False,
    )
```

time: 116 us -> 111 us (0.957)
  Pallas kernels: 115 us -> 110 us
    pallas_call x1, Pallas kernels: 109 us -> 104 us  [local(): pl.pallas_call(transfers, out_shape=(shape((ROWS, W), BF), shape((2, 2, N...]
where the time goes in v3:
time: 111 us
  Pallas kernels  110 us (99%)
    pallas_call x1, Pallas kernels, local(): pl.pallas_call(transfers, out_shape=(shape((ROWS, W), BF), shape((2, 2, N...  104 us
    pallas_call x1, Pallas kernels, local(): pl.pallas_call(outputs, out_shape=(shape((ROWS, W), BF), shape((2, 2, C,...  5.8 us

profile of v3, /device:TPU:1, one launch (start us, length us, event | category | flops | bytes accessed | tf_op | source)
XLA Modules:
  0.0 110.8 jit_solution(12774561460318059311)
XLA Ops:
  0.6 104.2 %transfers.1 = (bf16[1024,1024]{1,0:T(8,128)(2,1)}, f32[2,2,16,4,128]{4,3,2,1,0:T(4,128)}, f32[2,2,64,128]{3,2,1,0:T(8,128)}) custom-call(bf16[1024,1024]{1,0:T(8,128)(2,1)} %bitcast.4, bf16[1024,1024]{1,0:T(8,128)(2,1)} %bitcast.5, bf16[2,2,64,64,64]{4,3,2,1,0:T(8,128)(2,1)} %w_hbm.1, bf16[1024,512]{1,0:T(8,128)(2,1)} %constant.16.clone.t1_hbm, ...), custom_call_target="tpu_custom_call" | custom-call | tf_op jit(solution)/shard_map/transfers/pallas_call | solution.py:590
  104.9 5.8 %outputs.1 = (bf16[1024,1024]{1,0:T(8,128)(2,1)}, f32[2,2,64,64,64]{4,3,2,1,0:T(8,128)}) custom-call(bf16[1024,1024]{1,0:T(8,128)(2,1)} %get-tuple-element.7.sg_in, f32[2,2,16,4,128]{4,3,2,1,0:T(4,128)} %get-tuple-element.8.xm_hbm, f32[2,2,64,128]{3,2,1,0:T(8,128)} %get-tuple-element.9.gm_hbm), custom_call_target="tpu_custom_call" | custom-call | tf_op jit(solution)/shard_map/outputs/pallas_call | solution.py:667

commit v4 on v3

--- a/solution.py
+++ b/solution.py
@@ -192,13 +192,9 @@
 
     load_t1.wait()
 
-    def first(ip):
-        for i2 in range(2):
-            part = pl.ds((2 * ip + i2) * CHUNK, CHUNK)
-            loads[2 * ip + i2].wait()
-            split_columns(0, ip, i2, x[part])
-
-    first(0)
+    for i in range(NI):
+        loads[i].wait()
+        split_columns(0, i // 2, i % 2, x[i * CHUNK : (i + 1) * CHUNK], 0, 1)
     pl.semaphore_wait(barrier, 2 * NQ - 1 + NZ - 1)
 
     def send_plane(out, into, s, r, rnd, u, ip):
@@ -439,14 +435,14 @@
         send_plane(a_out, a_in, sa, ra, rnd, n // 2, n % 2)
 
     send_plane(a_out, a_in, sa, ra, 0, 0, 0)
-    first(1)
     send_plane(a_out, a_in, sa, ra, 0, 0, 1)
+    for i in range(NI):
+        split_columns(0, i // 2, i % 2, x[i * CHUNK : (i + 1) * CHUNK], 1, NU)
     load_w.wait()
     for copy in smalls:
         copy.wait()
-    loop(0, 16, widen)
     next_piece(0, 2)
-    loop(16, 32, widen)
+    loop(0, 32, widen)
     next_piece(0, 3)
     load_rows.wait()
     to_modes(0, 0, 0, 1)

time: 111 us -> 112 us (level)
    pallas_call x1, Pallas kernels: 104 us -> 106 us  [local(): pl.pallas_call(transfers, out_shape=(shape((ROWS, W), BF), shape((2, 2, N...]
where the time goes in v4:
time: 112 us
  Pallas kernels  111 us (99%)
    pallas_call x1, Pallas kernels, local(): pl.pallas_call(transfers, out_shape=(shape((ROWS, W), BF), shape((2, 2, N...  106 us
    pallas_call x1, Pallas kernels, local(): pl.pallas_call(outputs, out_shape=(shape((ROWS, W), BF), shape((2, 2, C,...  5.8 us

profile of v4, /device:TPU:1, one launch (start us, length us, event | category | flops | bytes accessed | tf_op | source)
XLA Modules:
  0.0 112.2 jit_solution(16011213161909171690)
XLA Ops:
  0.6 105.6 %transfers.1 = (bf16[1024,1024]{1,0:T(8,128)(2,1)}, f32[2,2,16,4,128]{4,3,2,1,0:T(4,128)}, f32[2,2,64,128]{3,2,1,0:T(8,128)}) custom-call(bf16[1024,1024]{1,0:T(8,128)(2,1)} %bitcast.4, bf16[1024,1024]{1,0:T(8,128)(2,1)} %bitcast.5, bf16[2,2,64,64,64]{4,3,2,1,0:T(8,128)(2,1)} %w_hbm.1, bf16[1024,512]{1,0:T(8,128)(2,1)} %constant.16.clone.t1_hbm, ...), custom_call_target="tpu_custom_call" | custom-call | tf_op jit(solution)/shard_map/transfers/pallas_call | solution.py:586
  106.2 5.8 %outputs.1 = (bf16[1024,1024]{1,0:T(8,128)(2,1)}, f32[2,2,64,64,64]{4,3,2,1,0:T(8,128)}) custom-call(bf16[1024,1024]{1,0:T(8,128)(2,1)} %get-tuple-element.7.sg_in, f32[2,2,16,4,128]{4,3,2,1,0:T(4,128)} %get-tuple-element.8.xm_hbm, f32[2,2,64,128]{3,2,1,0:T(8,128)} %get-tuple-element.9.gm_hbm), custom_call_target="tpu_custom_call" | custom-call | tf_op jit(solution)/shard_map/outputs/pallas_call | solution.py:663
